TPU v7x, 512 devices: a whole 4x8x8 slice. The times are simulated.
512 devices in a mesh: rows: 128 (over z, y, core), grp: 4 (over x).
Axes of the slice: x: 4, y: 8, z: 8, core: 2. Of those that a mesh axis runs over, the one named last changes fastest.
Arguments:
- owner: int32 [16384, 24, 3], P('rows', 'grp'), may hold values from 0 to 127, as said below
- offset: int32 [16384, 24, 3], P('rows', 'grp'), may hold values from 0 to 511
- tables: float32 [12, 65536, 128], P('grp', 'rows'), may hold values from -6 to 6
- w_first: bfloat16 [3072, 1024], P('grp'), may hold values from -0.109375 to 0.109375
- b_first: float32 [1024], replicated, may hold values from -3 to 3
- w_out: float32 [1024], replicated, may hold values from -0.1875 to 0.1875
- labels: int32 [16384], P('rows'), may hold values 0 or 1
Outputs:
- table_grad: float32 [12, 65536, 128], P('grp', 'rows')
- losses: float32 [16384], P(('rows', 'grp'))
Inputs may be any that keep to these rules, and one draw needn't show every extreme that they name: Of the lookups of one device (its 128 samples and 6 features, all three hashes) at most 72 name one owner, and in every draw some owner gets exactly 72. Among the lookups of one device to one owner for one table, at most 8 distinct offsets occur, and that bound is reached in every draw.
All inputs are finite; a program needn't handle non-finite values. No bound on the sum of `labels` on one device may be relied on, other than what follows from the above.
Results may differ from a plain program's by a relative error of at most 0.005.
Values may be sent and summed in bfloat16 or wider, within the bound.
No kernel may reach another device: no remote copies, remote signals or barrier semaphores. Data moves between devices by JAX's collectives and lax.ppermute only.
A program may use at most 64 MiB of HBM per device.

v0:
```python
import jax
import jax.numpy as jnp
from jax import lax
from jax.sharding import PartitionSpec as P


def split_up(array, dim, size):
    before, after = (array.shape[:dim], array.shape[dim + 1 :])
    return jnp.moveaxis(array.reshape(*before, size, -1, *after), dim, 0)


def sum_at_owner(array, axis, dim):
    parts = split_up(array, dim, lax.axis_size(axis))
    arrived = lax.all_to_all(parts, axis, split_axis=0, concat_axis=0, tiled=True)
    return arrived.sum(axis=0)


def copy_for_each(array, axis):
    size = lax.axis_size(axis)
    return lax.all_to_all(
        jnp.broadcast_to(array[None], (size, *array.shape)), axis, 0, 0, tiled=True
    )


def in_order(parts, dim):
    shape = list(parts.shape[1:])
    shape[dim] *= parts.shape[0]
    return jnp.moveaxis(parts, 0, dim).reshape(shape)


def collect(array, axis, dim):
    parts = copy_for_each(array, axis)
    return in_order(parts, dim)


def head_loss(pre_act, w_out, targets):
    gate_sig = jax.nn.sigmoid(pre_act)
    logits = jnp.sum(pre_act * gate_sig * w_out, axis=1)
    losses = jax.nn.softplus(logits) - targets * logits
    grad_logit = jax.nn.sigmoid(logits) - targets
    grad_pre = (
        grad_logit[:, None] * w_out * (gate_sig * (1.0 + pre_act * (1.0 - gate_sig)))
    ).astype(jnp.bfloat16)
    return (losses, grad_pre)


def run_starts(sorted_values, values_index):
    is_first = jnp.concatenate([jnp.ones((1,), bool), sorted_values[1:] != sorted_values[:-1]])
    return lax.cummax(jnp.where(is_first, values_index, 0), axis=0)


def body(owner, offset, tables, w_first, b_first, w_out, labels):
    row_devices = lax.axis_size("rows")
    bdev_rows, fgrp_count = (owner.shape[0], owner.shape[1])
    rows_dev, emb_width = (tables.shape[1], tables.shape[2])
    lookups = bdev_rows * fgrp_count * 3
    hot_count = 8 * (bdev_rows * fgrp_count * 7 // (16 * row_devices)) + 8
    owner_flat = owner.reshape(-1)
    offset_flat = offset.reshape(-1)
    positions = jnp.arange(lookups, dtype=jnp.int32)
    table_kind = positions % 3
    flat_table = tables.reshape(3 * rows_dev, emb_width)
    unique_cap = hot_count // 3
    group_key = (owner_flat * 3 + table_kind) * rows_dev + offset_flat
    ordering = jnp.argsort(group_key, stable=True)
    sorted_keys = group_key[ordering]
    is_new = jnp.concatenate([jnp.ones((1,), bool), sorted_keys[1:] != sorted_keys[:-1]])
    unique_id = jnp.cumsum(is_new.astype(jnp.int32)) - 1
    sorted_group = sorted_keys // rows_dev
    slot_sorted = sorted_group * unique_cap + unique_id - run_starts(sorted_group, unique_id)
    slot_of = jnp.zeros((lookups,), jnp.int32).at[ordering].set(slot_sorted)
    outgoing = jnp.full((row_devices * 3 * unique_cap,), -1, jnp.int32).at[slot_of].set(offset_flat)
    row_codes = lax.all_to_all(
        outgoing.reshape(row_devices, 3, unique_cap),
        "rows",
        split_axis=0,
        concat_axis=0,
        tiled=True,
    )
    is_live = (row_codes >= 0)[..., None]
    row_index = jnp.arange(3, dtype=jnp.int32)[None, :, None] * rows_dev + jnp.maximum(row_codes, 0)
    fetched = jnp.take(flat_table, row_index.reshape(-1), axis=0)
    fetched = (fetched.reshape(row_codes.shape + (emb_width,)) * is_live).astype(jnp.bfloat16)
    returned = lax.all_to_all(fetched, "rows", split_axis=0, concat_axis=0, tiled=True)
    owner_codes, returned = (row_codes, returned)
    owner_index = (
        jnp.arange(3, dtype=jnp.int32)[None, :, None] * rows_dev + jnp.maximum(owner_codes, 0)
    ).reshape(-1)
    looked = (
        returned.reshape(-1, emb_width)[slot_of]
        .astype(jnp.float32)
        .reshape(bdev_rows, fgrp_count, 3, emb_width)
    )
    embedded = looked[:, :, 0] * looked[:, :, 1] + looked[:, :, 2]
    features = embedded.reshape(bdev_rows, fgrp_count * emb_width).astype(jnp.bfloat16)
    targets = labels.astype(jnp.float32)
    share_rows = bdev_rows // lax.axis_size("grp")
    share_start = lax.axis_index("grp") * share_rows
    pre_share = (
        sum_at_owner(jnp.dot(features, w_first, preferred_element_type=jnp.float32), "grp", 0)
        + b_first
    )
    share_targets = lax.dynamic_slice_in_dim(targets, share_start, share_rows, 0)
    losses, grad_share = head_loss(pre_share, w_out, share_targets)
    grad_pre = collect(grad_share, "grp", 0)
    grad_emb = jnp.dot(grad_pre, w_first.T, preferred_element_type=jnp.float32).reshape(
        bdev_rows, fgrp_count, emb_width
    )
    row_grads = jnp.stack(
        [grad_emb * looked[:, :, 1], grad_emb * looked[:, :, 0], grad_emb], axis=2
    ).reshape(lookups, emb_width)
    outgoing_grads = (
        jnp.zeros((row_devices * 3 * unique_cap, emb_width), jnp.float32).at[slot_of].add(row_grads)
    )
    received = lax.all_to_all(
        outgoing_grads.reshape(row_devices, 3, unique_cap, emb_width),
        "rows",
        split_axis=0,
        concat_axis=0,
        tiled=True,
    )
    table_grad = (
        jnp.zeros((3 * rows_dev, emb_width), jnp.float32)
        .at[owner_index]
        .add(received.reshape(-1, emb_width))
    )
    return (table_grad.reshape(3, rows_dev, emb_width), losses)


def solution(mesh):
    placed = (
        P("rows", "grp", None),
        P("rows", "grp", None),
        P("grp", "rows", None),
        P("grp", None),
        P(),
        P(),
        P("rows"),
    )
    return jax.shard_map(
        body,
        mesh=mesh,
        in_specs=placed,
        out_specs=(P("grp", "rows", None), P(("rows", "grp"))),
        check_vma=False,
    )
```

profile of v0, /device:TPU:1, one launch (start us, length us, event | category | flops | bytes accessed | tf_op | source)
XLA Modules:
  0.0 240.8 jit_solution(8865204127160990035)
XLA Ops:
  0.6 0.8 broadcast_multiply_fusion
  1.5 0.3 copy.27
  1.9 1.0 copy.28
  3.1 5.8 %sort.17 = (s32[2304]{0:T(1024)}, s32[2304]{0:T(1024)S(1)}) sort(s32[2304]{0:T(1024)S(1)} %fusion.9, s32[2304]{0:T(1024)S(1)} %iota.15), dimensions={0}, to_apply=%region_0.1 | sort | flops 27648 | bytes 36864 | tf_op jit(solution)/shard_map/jit(argsort)/sort | solution.py:65
  8.9 12.3 %gather_fusion = s32[2304]{0:T(1024)S(1)} fusion(s32[2304]{0:T(1024)S(1)} %fusion.9, s32[3072]{0:T(1024)S(1)} %pad_clamp_fusion.1), kind=kCustom, calls=%fused_computation | custom fusion | bytes 27648 | tf_op jit(solution)/shard_map/gather | solution.py:66
  21.4 0.3 reduce-window.16
  22.1 0.3 reduce-window.24
  22.7 9.0 %scatter_custom_fusion = s32[2304]{0:T(1024)S(1)} fusion(s32[2304]{0:T(1024)S(1)} %compare_select_fusion.3, s32[2304]{0:T(1024)S(1)} %bitcast_subtract_fusion, s32[]{:T(128)} %constant.33.clone.1), kind=kCustom, calls=%fused_computation.61 | custom fusion | bytes 9220 | tf_op jit(solution)/shard_map/scatter | solution.py:71
  31.7 9.0 %scatter_custom_fusion.1 = s32[3072]{0:T(1024)S(1)} fusion(s32[2304]{0:T(1024)S(1)} %compare_select_fusion.2, s32[2304]{0:T(1024)S(1)} %reshape.246, s32[]{:T(128)} %constant.31.clone.1), kind=kCustom, calls=%fused_computation.63 | custom fusion | bytes 12292 | tf_op jit(solution)/shard_map/scatter | solution.py:72
  40.7 0.9 reshape.198
  41.6 18.4 %all-to-all-start = ((s32[128,3,8]{2,1,0:T(4,128)}), s32[128,3,8]{2,1,0:T(4,128)S(1)}, u32[]{:S(2)}, u32[]{:S(2)}) async-start(s32[128,3,8]{2,1,0:T(4,128)} %reshape.198), calls=%async_computation | async-start | bytes 524288 | tf_op jit(solution)/shard_map/all_to_all | solution.py:73
  60.0 15.2 %all-to-all-done = s32[128,3,8]{2,1,0:T(4,128)S(1)} async-done(((s32[128,3,8]{2,1,0:T(4,128)}), s32[128,3,8]{2,1,0:T(4,128)S(1)}, u32[]{:S(2)}, u32[]{:S(2)}) %all-to-all-start) | async-done | bytes 12320 | tf_op jit(solution)/shard_map/all_to_all | solution.py:73
  76.0 0.6 copy-done.4
  76.8 10.8 %gather_fusion.1 = f32[3072,128]{1,0:T(8,128)} fusion(f32[1536,128]{1,0:T(8,128)S(1)} %bitcast.36, s32[3072]{0:T(1024)S(1)} %broadcast_clamp_fusion), kind=kCustom, calls=%fused_computation.1 | custom fusion | bytes 3158016 | tf_op jit(solution)/shard_map/jit(_take)/gather | solution.py:82
  87.6 3.6 %multiply_convert_fusion = bf16[128,3,8,128]{3,2,1,0:T(8,128)(2,1)} fusion(f32[128,3,8,128]{3,2,1,0:T(8,128)} %bitcast.38, f32[128,3,8]{2,1,0:T(4,128)S(1)} %copy.33, pred[128,3,8]{2,1,0:T(4,128)(4,1)S(1)} %copy.31), kind=kLoop, calls=%fused_computation.9 | loop fusion | flops 1179648 | bytes 2374656 | tf_op jit(solution)/shard_map/convert_element_type | solution.py:83
  91.2 5.6 %all-to-all-start.1 = ((bf16[128,3,8,128]{3,2,1,0:T(8,128)(2,1)}), bf16[128,3,8,128]{3,2,1,0:T(8,128)(2,1)S(1)}, u32[]{:S(2)}, u32[]{:S(2)}) async-start(bf16[128,3,8,128]{3,2,1,0:T(8,128)(2,1)} %multiply_convert_fusion), calls=%async_computation.1 | async-start | bytes 1572864 | tf_op jit(solution)/shard_map/all_to_all | solution.py:84
  96.7 26.0 %all-to-all-done.1 = bf16[128,3,8,128]{3,2,1,0:T(8,128)(2,1)S(1)} async-done(((bf16[128,3,8,128]{3,2,1,0:T(8,128)(2,1)}), bf16[128,3,8,128]{3,2,1,0:T(8,128)(2,1)S(1)}, u32[]{:S(2)}, u32[]{:S(2)}) %all-to-all-start.1) | async-done | bytes 786464 | tf_op jit(solution)/shard_map/all_to_all | solution.py:84
  122.8 5.6 %gather_fusion.2 = bf16[2304,128]{1,0:T(8,128)(2,1)} fusion(bf16[3072,128]{1,0:T(8,128)(2,1)S(1)} %bitcast.37, s32[3072]{0:T(1024)S(1)} %pad_clamp_fusion), kind=kCustom, calls=%fused_computation.2 | custom fusion | bytes 1188864 | tf_op jit(solution)/shard_map/gather | solution.py:90
  128.3 2.0 reshape.209
  130.4 0.8 fusion.22
  131.2 0.7 copy-done.2
  132.5 1.2 fusion
  133.6 4.1 %all-to-all-start.2 = ((f32[4,32,1024]{2,1,0:T(8,128)}), f32[4,32,1024]{2,1,0:T(8,128)S(1)}, u32[]{:S(2)}, u32[]{:S(2)}) async-start(f32[4,32,1024]{2,1,0:T(8,128)} %fusion), calls=%async_computation.2 | async-start | bytes 1048576 | tf_op jit(solution)/shard_map/all_to_all | solution.py:14
  137.8 9.5 %all-to-all-done.2 = f32[4,32,1024]{2,1,0:T(8,128)S(1)} async-done(((f32[4,32,1024]{2,1,0:T(8,128)}), f32[4,32,1024]{2,1,0:T(8,128)S(1)}, u32[]{:S(2)}, u32[]{:S(2)}) %all-to-all-start.2) | async-done | bytes 524320 | tf_op jit(solution)/shard_map/all_to_all | solution.py:14
  147.5 0.6 fusion.21
  148.2 7.9 %all_to_all.25 = bf16[4,32,1024]{2,1,0:T(8,128)(2,1)S(1)} all-to-all(bf16[4,32,1024]{2,1,0:T(8,128)(2,1)S(1)} %broadcast_in_dim.51), channel_id=1, replica_groups=mesh['rows'=128,'grp'=4] {'grp'}, dimensions={0} | all-to-all | bytes 524288 | tf_op jit(solution)/shard_map/all_to_all | solution.py:20
  156.1 0.7 copy_multiply_fusion
  156.9 0.8 copy.38
  157.7 1.4 reshape.254
  159.1 15.0 %scatter_custom_fusion.2 = f32[3072,128]{1,0:T(8,128)S(1)} fusion(s32[2304]{0:T(1024)S(1)} %compare_select_fusion.2, f32[2304,128]{1,0:T(8,128)} %reshape.254, f32[]{:T(128)} %constant.26.clone.1), kind=kCustom, calls=%fused_computation.12 | custom fusion | flops 294912 | bytes 1573376 | tf_op jit(solution)/shard_map/scatter-add | solution.py:113
  174.1 48.6 %all_to_all.26 = f32[128,3,8,128]{3,2,1,0:T(8,128)} all-to-all(f32[128,3,8,128]{3,2,1,0:T(8,128)S(1)} %bitcast.39), channel_id=1, replica_groups=mesh['rows'=128,'grp'=4] {'rows'}, dimensions={0} | all-to-all | bytes 3145728 | tf_op jit(solution)/shard_map/all_to_all | solution.py:115
  222.7 18.1 %scatter_custom_fusion.3 = f32[1536,128]{1,0:T(8,128)} fusion(s32[3072]{0:T(1024)} %bitcast.44, f32[3072,128]{1,0:T(8,128)} %bitcast.40, f32[]{:T(128)} %constant.26.clone.1), kind=kCustom, calls=%fused_computation.16 | custom fusion | flops 393216 | bytes 786944 | tf_op jit(solution)/shard_map/scatter-add | solution.py:125
  (52 shorter events, 3.0 us)
Async XLA Ops:
  0.6 131.8 %copy-start = (bf16[768,1024]{1,0:T(8,128)(2,1)S(1)}, bf16[768,1024]{1,0:T(8,128)(2,1)}, u32[]{:S(2)}) copy-start(bf16[768,1024]{1,0:T(8,128)(2,1)} %param.10) | copy-start | bytes 4718596
  21.2 55.5 %copy-start.1 = (f32[3,512,128]{2,1,0:T(8,128)S(1)}, f32[3,512,128]{2,1,0:T(8,128)}, u32[]{:S(2)}) copy-start(f32[3,512,128]{2,1,0:T(8,128)} %param.9) | copy-start | bytes 2359300
  41.6 33.7 %all-to-all-start = ((s32[128,3,8]{2,1,0:T(4,128)}), s32[128,3,8]{2,1,0:T(4,128)S(1)}, u32[]{:S(2)}, u32[]{:S(2)}) async-start(s32[128,3,8]{2,1,0:T(4,128)} %reshape.198), calls=%async_computation | async-start | bytes 524288 | tf_op jit(solution)/shard_map/all_to_all | solution.py:73
  76.0 0.6 copy-start.4
  91.2 31.6 %all-to-all-start.1 = ((bf16[128,3,8,128]{3,2,1,0:T(8,128)(2,1)}), bf16[128,3,8,128]{3,2,1,0:T(8,128)(2,1)S(1)}, u32[]{:S(2)}, u32[]{:S(2)}) async-start(bf16[128,3,8,128]{3,2,1,0:T(8,128)(2,1)} %multiply_convert_fusion), calls=%async_computation.1 | async-start | bytes 1572864 | tf_op jit(solution)/shard_map/all_to_all | solution.py:84
  131.2 0.7 copy-start.2
  132.4 5.4 %copy-start.7 = (s32[128]{0:T(128)S(1)}, s32[128]{0:T(128)}, u32[]{:S(2)}) copy-start(s32[128]{0:T(128)} %param.13) | copy-start | bytes 1540
  132.4 14.9 %copy-start.5 = (f32[1024]{0:T(1024)S(1)}, f32[1024]{0:T(1024)}, u32[]{:S(2)}) copy-start(f32[1024]{0:T(1024)} %param.12) | copy-start | bytes 12292
  132.4 14.9 %copy-start.6 = (f32[1024]{0:T(1024)S(1)}, f32[1024]{0:T(1024)}, u32[]{:S(2)}) copy-start(f32[1024]{0:T(1024)} %param.11) | copy-start | bytes 12292
  133.6 22.5 %copy-start.3 = (f32[128,6,1,128]{3,2,1,0:T(1,128)S(1)}, f32[128,6,1,128]{3,2,1,0:T(1,128)}, u32[]{:S(2)}) copy-start(f32[128,6,1,128]{3,2,1,0:T(1,128)} %copy-done.2) | copy-start | bytes 1179652
  133.6 13.6 %all-to-all-start.2 = ((f32[4,32,1024]{2,1,0:T(8,128)}), f32[4,32,1024]{2,1,0:T(8,128)S(1)}, u32[]{:S(2)}, u32[]{:S(2)}) async-start(f32[4,32,1024]{2,1,0:T(8,128)} %fusion), calls=%async_computation.2 | async-start | bytes 1048576 | tf_op jit(solution)/shard_map/all_to_all | solution.py:14
where the time goes:
time: 242 us; the launch traced here: 241 us
  local copies, waits for them, and re-layouts  57.1 us (24%)
  blocking collectives  56.6 us (23%)
  waiting for transfers between devices  50.7 us (21%)
  other arithmetic  45.5 us (19%)
  starting transfers between devices  28.1 us (12%)
    all_to_all x1, blocking collectives, body(): lax.all_to_all(outgoing_grads.reshape(row_devices, 3, unique_cap, emb_wid...  48.6 us
    all_to_all x1, waiting for transfers between devices, body(): lax.all_to_all(fetched, 'rows', split_axis=0, concat_axis=0, tiled=True)  26 us
    all_to_all x1, starting transfers between devices, body(): lax.all_to_all(outgoing.reshape(row_devices, 3, unique_cap), 'rows', spli...  18.4 us
    scatter-add x1, other arithmetic, body(): table_grad = jnp.zeros((3 * rows_dev, emb_width), jnp.float32).at[owner_i...  18.1 us
    all_to_all x1, waiting for transfers between devices, body(): lax.all_to_all(outgoing.reshape(row_devices, 3, unique_cap), 'rows', spli...  15.2 us
    scatter-add x1, other arithmetic, body(): jnp.zeros((row_devices * 3 * unique_cap, emb_width), jnp.float32)  15 us
    gather x1, local copies, waits for them, and re-layouts, body(): sorted_keys = group_key[ordering]  12.3 us
    gather x1, local copies, waits for them, and re-layouts, body(): fetched = jnp.take(flat_table, row_index.reshape(-1), axis=0)  10.8 us
  transfers between devices with their start and end apart: 3, of which 3 were waited for; matrix products, arithmetic and copies ran while one was open for 0% of the time, Pallas kernels for 0%

commit v1 on v0

v1 whole, which is shorter than its diff:
```python
import functools

import jax
import jax.numpy as jnp
from jax import lax
from jax.experimental import pallas as pl
from jax.experimental.pallas import tpu as pltpu
from jax.sharding import PartitionSpec as P

SLOTS = 8
LANES = 128
VMEM = 40 * 2**20
BF16 = jnp.bfloat16
F32 = jnp.float32


def dot(a, b, ca, cb):
    return lax.dot_general(a, b, (((ca,), (cb,)), ((), ())), preferred_element_type=F32)


def iota(shape, dim):
    return lax.broadcasted_iota(jnp.int32, shape, dim)


def hot(mask):
    return jnp.where(mask, 1.0, 0.0).astype(BF16)


def call(kernel, out_shape, flops=0, n_in=1, scalars=()):
    specs = [
        pl.BlockSpec(memory_space=pltpu.SMEM if i in scalars else pltpu.VMEM) for i in range(n_in)
    ]
    return pl.pallas_call(
        kernel,
        out_shape=out_shape,
        in_specs=specs,
        compiler_params=pltpu.CompilerParams(vmem_limit_bytes=VMEM),
        cost_estimate=pl.CostEstimate(flops=flops, bytes_accessed=2**20, transcendentals=0),
    )


def index_kernel(rows_dev, codes_ref, cols_ref, out_ref):
    n_owner = out_ref.shape[0]
    n_look = codes_ref.shape[1]
    before = hot(iota((rows_dev, rows_dev), 0) < iota((rows_dev, rows_dev), 1))
    offsets = iota((n_owner, rows_dev), 1)
    lane = iota((n_owner, LANES), 1)
    asked = jnp.full((n_owner, LANES), -1, jnp.int32)
    for k in range(3):
        code = codes_ref[k : k + 1, :]
        owner = code // rows_dev
        offset = code - owner * rows_dev
        owner_hot = hot(iota((n_owner, n_look), 0) == owner)
        offset_hot = hot(iota((rows_dev, n_look), 0) == offset)
        present = dot(owner_hot, offset_hot, 1, 1) > 0.5
        rank = dot(hot(present), before, 1, 0)
        at_owner = dot(rank.astype(BF16), offset_hot, 1, 0)
        slot = jnp.sum(owner_hot.astype(F32) * at_owner, axis=0, keepdims=True)
        cols_ref[k : k + 1, :] = owner * SLOTS + slot.astype(jnp.int32)
        rank = jnp.where(present, rank.astype(jnp.int32), -1)
        for s in range(SLOTS):
            found = jnp.where(rank == s, offsets + 1, 0).astype(F32)
            found = jnp.sum(found, axis=1, keepdims=True).astype(jnp.int32) - 1
            asked = jnp.where(lane == k * SLOTS + s, found, asked)
    out_ref[...] = asked


def request_column(codes, k):
    n_src = codes.shape[0]
    wide = jnp.broadcast_to(codes[:, None, :].astype(F32), (n_src, SLOTS, LANES))
    mine = iota((1, SLOTS, LANES), 2) == iota((1, SLOTS, LANES), 1) + k * SLOTS
    column = jnp.sum(jnp.where(mine, wide, 0.0), axis=2, keepdims=True)
    return column.reshape(n_src * SLOTS, 1).astype(jnp.int32)


def fetch_kernel(codes_ref, table_ref, out_ref):
    n_src = codes_ref.shape[0]
    rows_dev = table_ref.shape[1]
    width = table_ref.shape[2]
    codes = codes_ref[...]
    parts = []
    for k in range(3):
        onehot = hot(iota((n_src * SLOTS, rows_dev), 1) == request_column(codes, k))
        rows = dot(onehot, table_ref[k].astype(BF16), 1, 0)
        parts.append(rows.reshape(n_src, SLOTS, width))
    rows = jnp.concatenate(parts, axis=1)
    out_ref[...] = rows.reshape(n_src * 3 * SLOTS, width).astype(BF16)


def forward_kernel(rows_ref, cols_ref, w_ref, pre_ref, looked_ref):
    width = rows_ref.shape[1]
    n_look = cols_ref.shape[1]
    n_owner = rows_ref.shape[0] // (3 * SLOTS)
    n_feat = w_ref.shape[0] // width
    rows = rows_ref[...].astype(F32).reshape(n_owner, 3 * SLOTS, width)
    looked = []
    for k in range(3):
        mine = rows[:, k * SLOTS : (k + 1) * SLOTS, :].reshape(n_owner * SLOTS, width).astype(BF16)
        onehot = hot(iota((n_owner * SLOTS, n_look), 0) == cols_ref[k : k + 1, :])
        looked.append(dot(mine, onehot, 0, 0))
    looked_ref[0] = looked[0].astype(BF16)
    looked_ref[1] = looked[1].astype(BF16)
    emb = (looked[0] * looked[1] + looked[2]).astype(BF16)
    n_b = n_look // n_feat
    emb = jnp.concatenate([emb[:, f * n_b : (f + 1) * n_b] for f in range(n_feat)], axis=0)
    pre_ref[...] = dot(emb, w_ref[...], 0, 0).astype(BF16)


def head_kernel(grp_ref, pre_ref, b_ref, w_out_ref, labels_ref, grad_ref, loss_ref):
    n_grp, share, _ = grad_ref.shape
    pre = b_ref[...]
    for g in range(n_grp):
        pre = pre + pre_ref[g * share : (g + 1) * share, :].astype(F32)
    w_out = w_out_ref[...]
    sig = jax.nn.sigmoid(pre)
    logits = jnp.sum(pre * sig * w_out, axis=1, keepdims=True)
    n_b = labels_ref.shape[1]
    mine = iota((share, n_b), 1) == iota((share, n_b), 0) + grp_ref[0] * share
    targets = jnp.sum(jnp.where(mine, labels_ref[...].astype(F32), 0.0), axis=1, keepdims=True)
    soft = jnp.maximum(logits, 0.0) + jnp.log1p(jnp.exp(-jnp.abs(logits)))
    losses = soft - targets * logits
    grad_logit = jax.nn.sigmoid(logits) - targets
    grad = (grad_logit * w_out * (sig * (1.0 + pre * (1.0 - sig)))).astype(BF16)
    for g in range(n_grp):
        grad_ref[g] = grad
    diagonal = iota((share, share), 0) == iota((share, share), 1)
    loss_ref[...] = jnp.sum(jnp.where(diagonal, losses, 0.0), axis=0, keepdims=True)


def backward_kernel(grad_ref, w_ref, cols_ref, looked_ref, out_ref):
    width = out_ref.shape[1]
    n_look = cols_ref.shape[1]
    n_owner = out_ref.shape[0] // (3 * SLOTS)
    n_feat = w_ref.shape[0] // width
    grad_t = dot(w_ref[...], grad_ref[...], 1, 1)
    emb_t = jnp.concatenate([grad_t[f * width : (f + 1) * width] for f in range(n_feat)], axis=1)
    factors = (looked_ref[1].astype(F32), looked_ref[0].astype(F32), None)
    parts = []
    for k in range(3):
        row_t = emb_t if factors[k] is None else emb_t * factors[k]
        high = row_t.astype(BF16)
        low = (row_t - high.astype(F32)).astype(BF16)
        onehot = hot(iota((n_owner * SLOTS, n_look), 0) == cols_ref[k : k + 1, :])
        sums = dot(onehot, jnp.concatenate([high, low], axis=0), 1, 1)
        sums = sums[:, :width] + sums[:, width:]
        parts.append(sums.reshape(n_owner, SLOTS, width))
    out_ref[...] = jnp.concatenate(parts, axis=1).reshape(n_owner * 3 * SLOTS, width).astype(BF16)


def owner_kernel(codes_ref, grads_ref, out_ref):
    n_src = codes_ref.shape[0]
    rows_dev, width = out_ref.shape[1:]
    codes = codes_ref[...]
    grads = grads_ref[...].astype(F32).reshape(n_src, 3 * SLOTS, width)
    for k in range(3):
        mine = grads[:, k * SLOTS : (k + 1) * SLOTS, :].reshape(n_src * SLOTS, width).astype(BF16)
        onehot = hot(iota((n_src * SLOTS, rows_dev), 1) == request_column(codes, k))
        out_ref[k] = dot(mine, onehot, 0, 0).T


def exchange(array, axis):
    return lax.all_to_all(array, axis, split_axis=0, concat_axis=0, tiled=True)


def body(owner, offset, tables, w_first, b_first, w_out, labels):
    n_rows = lax.axis_size("rows")
    n_grp = lax.axis_size("grp")
    n_b, n_feat = owner.shape[:2]
    rows_dev, width = tables.shape[1:]
    hidden = w_first.shape[1]
    n_look = n_b * n_feat
    shape = jax.ShapeDtypeStruct
    codes = (owner * rows_dev + offset).transpose(2, 1, 0).reshape(3, n_look)
    cols, asked = call(
        functools.partial(index_kernel, rows_dev),
        (shape((3, n_look), jnp.int32), shape((n_rows, LANES), jnp.int32)),
    )(codes)
    requests = exchange(asked, "rows")
    rows = call(fetch_kernel, shape((n_rows * 3 * SLOTS, width), BF16), n_in=2)(requests, tables)
    rows = exchange(rows, "rows")
    pre, looked = call(
        forward_kernel,
        (shape((n_b, hidden), BF16), shape((2, width, n_look), BF16)),
        n_in=3,
    )(rows, cols, w_first)
    pre = exchange(pre, "grp")
    grp = lax.axis_index("grp").astype(jnp.int32).reshape(1)
    share = n_b // n_grp
    grad, losses = call(
        head_kernel,
        (shape((n_grp, share, hidden), BF16), shape((1, share), F32)),
        n_in=5,
        scalars=(0,),
    )(grp, pre, b_first.reshape(1, hidden), w_out.reshape(1, hidden), labels.reshape(1, n_b))
    grad = exchange(grad.reshape(n_b, hidden), "grp")
    sums = call(backward_kernel, shape((n_rows * 3 * SLOTS, width), BF16), n_in=4)(
        grad, w_first, cols, looked
    )
    sums = exchange(sums, "rows")
    table_grad = call(owner_kernel, shape((3, rows_dev, width), F32), n_in=2)(requests, sums)
    return table_grad, losses.reshape(share)


def solution(mesh):
    placed = (
        P("rows", "grp", None),
        P("rows", "grp", None),
        P("grp", "rows", None),
        P("grp", None),
        P(),
        P(),
        P("rows"),
    )
    return jax.shard_map(
        body,
        mesh=mesh,
        in_specs=placed,
        out_specs=(P("grp", "rows", None), P(("rows", "grp"))),
        check_vma=False,
    )
```

time: 242 us -> 127 us (0.52)
  local copies, waits for them, and re-layouts: 57.1 us -> 1.15 us
  blocking collectives: 56.6 us -> 102 us
  other arithmetic: 45.5 us -> 0.73 us
  waiting for transfers between devices: 50.7 us -> 6.67 us
  starting transfers between devices: 28.1 us -> 4.02 us
  Pallas kernels: 0 us -> 12.2 us
    all_to_all x2 -> x4, blocking collectives: 56.6 us -> 102 us  [exchange(): return lax.all_to_all(array, axis, split_axis=0, concat_axis=0, tiled=True)]
    all_to_all x3 -> x1, waiting for transfers between devices: 50.7 us -> 6.67 us  [exchange(): return lax.all_to_all(array, axis, split_axis=0, concat_axis=0, tiled=True)]
    scatter-add x2 -> x0, other arithmetic: 33.1 us -> none  [the longest x1 18.1 us: body(): table_grad = jnp.zeros((3 * rows_dev, emb_width), jnp.float32).at[owner_i...]
    gather x3 -> x0, local copies, waits for them, and re-layouts: 28.7 us -> none  [the longest x1 12.3 us: body(): sorted_keys = group_key[ordering]]
    all_to_all x3 -> x1, starting transfers between devices: 28.1 us -> 4.02 us  [exchange(): return lax.all_to_all(array, axis, split_axis=0, concat_axis=0, tiled=True)]
    scatter x2 -> x0, local copies, waits for them, and re-layouts: 18 us -> none  [the longest x1 9 us: body(): slot_of = jnp.zeros((lookups,), jnp.int32).at[ordering].set(slot_sorted)]
    pallas_call x0 -> x6, Pallas kernels: none -> 12.2 us  [the longest x1 2.7 us: body(): call(functools.partial(index_kernel, rows_dev), (shape((3, n_look), jnp.i...]
    sort x1 -> x0, other arithmetic: 5.76 us -> none  [body(): ordering = jnp.argsort(group_key, stable=True)]
  transfers between devices with their start and end apart: 3 -> 1, of which waited for: 3 -> 1; matrix products, arithmetic and copies ran while one was open for 0% -> 0% of each run, Pallas kernels for 0% -> 0%
where the time goes in v1:
time: 127 us
  blocking collectives  102 us (80%)
  Pallas kernels  12.2 us (10%)
  waiting for transfers between devices  6.67 us (5%)
  starting transfers between devices  4.02 us (3%)
    all_to_all x4, blocking collectives, exchange(): return lax.all_to_all(array, axis, split_axis=0, concat_axis=0, tiled=True)  102 us
    all_to_all x1, waiting for transfers between devices, exchange(): return lax.all_to_all(array, axis, split_axis=0, concat_axis=0, tiled=True)  6.67 us
    all_to_all x1, starting transfers between devices, exchange(): return lax.all_to_all(array, axis, split_axis=0, concat_axis=0, tiled=True)  4.02 us
    pallas_call x1, Pallas kernels, body(): call(functools.partial(index_kernel, rows_dev), (shape((3, n_look), jnp.i...  2.7 us
    pallas_call x1, Pallas kernels, body(): call(owner_kernel, shape((3, rows_dev, width), F32), n_in=2)(requests, sums)  2.7 us
    pallas_call x1, Pallas kernels, body(): call(backward_kernel, shape((n_rows * 3 * SLOTS, width), BF16), n_in=4)  2.64 us
  transfers between devices with their start and end apart: 1, of which 1 were waited for; matrix products, arithmetic and copies ran while one was open for 0% of the time, Pallas kernels for 0%

profile of v1, /device:TPU:1, one launch (start us, length us, event | category | flops | bytes accessed | tf_op | source)
XLA Modules:
  0.0 127.0 jit_solution(18385684526336467964)
XLA Ops:
  0.6 0.7 add_bitcast_fusion.codes_ref
  1.4 2.7 %shard_map.86 = (s32[3,768]{1,0:T(4,128)S(1)}, s32[128,128]{1,0:T(8,128)S(1)}) custom-call(s32[3,768]{1,0:T(4,128)S(1)} %add_bitcast_fusion.codes_ref), custom_call_target="tpu_custom_call" | custom-call | bytes 1048576 | tf_op jit(solution)/shard_map/pallas_call | solution.py:174
  4.1 29.7 %all_to_all.52 = s32[128,1,128]{2,1,0:T(1,128)S(1)} all-to-all(s32[128,1,128]{2,1,0:T(1,128)S(1)} %bitcast.28), channel_id=1, replica_groups=mesh['rows'=128,'grp'=4] {'rows'}, dimensions={0} | all-to-all | bytes 131072 | tf_op jit(solution)/shard_map/all_to_all | solution.py:162
  33.7 0.0 copy-start.1
  33.7 1.1 copy-done.1
  34.9 0.0 copy-start
  34.9 1.3 %shard_map.87 = bf16[3072,128]{1,0:T(8,128)(2,1)S(1)} custom-call(s32[128,128]{1,0:T(8,128)S(1)} %bitcast.26, f32[3,512,128]{2,1,0:T(8,128)S(1)} %copy-done.1), custom_call_target="tpu_custom_call" | custom-call | bytes 1048576 | tf_op jit(solution)/shard_map/pallas_call | solution.py:179
  36.2 31.1 %all_to_all.53 = bf16[128,24,128]{2,1,0:T(8,128)(2,1)S(1)} all-to-all(bf16[128,24,128]{2,1,0:T(8,128)(2,1)S(1)} %bitcast.21), channel_id=1, replica_groups=mesh['rows'=128,'grp'=4] {'rows'}, dimensions={0} | all-to-all | bytes 1572864 | tf_op jit(solution)/shard_map/all_to_all | solution.py:162
  67.3 0.0 copy-start.2
  67.3 0.0 copy-start.3
  67.3 0.0 copy-start.4
  67.3 0.0 copy-done
  67.3 2.2 %shard_map.88 = (bf16[128,1024]{1,0:T(8,128)(2,1)}, bf16[2,128,768]{2,1,0:T(8,128)(2,1)S(1)}) custom-call(bf16[3072,128]{1,0:T(8,128)(2,1)S(1)} %bitcast.22, s32[3,768]{1,0:T(4,128)S(1)} %get-tuple-element.9.cols_ref, bf16[768,1024]{1,0:T(8,128)(2,1)S(1)} %copy-done), custom_call_target="tpu_custom_call" | custom-call | bytes 1048576 | tf_op jit(solution)/shard_map/pallas_call | solution.py:181
  69.5 4.0 %all-to-all-start.2 = ((bf16[4,32,1024]{2,1,0:T(8,128)(2,1)}), bf16[4,32,1024]{2,1,0:T(8,128)(2,1)S(1)}, u32[]{:S(2)}, u32[]{:S(2)}) async-start(bf16[4,32,1024]{2,1,0:T(8,128)(2,1)} %bitcast.8), calls=%async_computation.2 | async-start | bytes 524288 | tf_op jit(solution)/shard_map/all_to_all | solution.py:162
  73.5 6.7 %all-to-all-done.2 = bf16[4,32,1024]{2,1,0:T(8,128)(2,1)S(1)} async-done(((bf16[4,32,1024]{2,1,0:T(8,128)(2,1)}), bf16[4,32,1024]{2,1,0:T(8,128)(2,1)S(1)}, u32[]{:S(2)}, u32[]{:S(2)}) %all-to-all-start.2) | async-done | bytes 262176 | tf_op jit(solution)/shard_map/all_to_all | solution.py:162
  80.2 0.0 copy-done.2
  80.2 0.0 copy-done.3
  80.2 0.0 copy-done.4
  80.2 0.7 shard_map.89
  80.9 7.9 %all_to_all.54 = bf16[4,32,1024]{2,1,0:T(8,128)(2,1)S(1)} all-to-all(bf16[4,32,1024]{2,1,0:T(8,128)(2,1)S(1)} %get-tuple-element.11), channel_id=1, replica_groups=mesh['rows'=128,'grp'=4] {'grp'}, dimensions={0} | all-to-all | bytes 524288 | tf_op jit(solution)/shard_map/all_to_all | solution.py:162
  88.8 2.6 %shard_map.90 = bf16[3072,128]{1,0:T(8,128)(2,1)S(1)} custom-call(bf16[128,1024]{1,0:T(8,128)(2,1)S(1)} %bitcast.24, bf16[768,1024]{1,0:T(8,128)(2,1)S(1)} %copy-done, s32[3,768]{1,0:T(4,128)S(1)} %get-tuple-element.9.cols_ref, bf16[2,128,768]{2,1,0:T(8,128)(2,1)S(1)} %get-tuple-element.12.looked_ref), custom_call_target="tpu_custom_call" | custom-call | bytes 1048576 | tf_op jit(solution)/shard_map/pallas_call | solution.py:196
  91.5 32.8 %all_to_all.55 = bf16[128,24,128]{2,1,0:T(8,128)(2,1)S(1)} all-to-all(bf16[128,24,128]{2,1,0:T(8,128)(2,1)S(1)} %bitcast.23), channel_id=1, replica_groups=mesh['rows'=128,'grp'=4] {'rows'}, dimensions={0} | all-to-all | bytes 1572864 | tf_op jit(solution)/shard_map/all_to_all | solution.py:162
  124.3 2.7 %shard_map.91 = f32[3,512,128]{2,1,0:T(8,128)} custom-call(s32[128,128]{1,0:T(8,128)S(1)} %bitcast.27, bf16[3072,128]{1,0:T(8,128)(2,1)S(1)} %bitcast.20), custom_call_target="tpu_custom_call" | custom-call | bytes 1048576 | tf_op jit(solution)/shard_map/pallas_call | solution.py:200
Async XLA Ops:
  33.7 1.1 copy-start.1
  34.9 32.4 %copy-start = (bf16[768,1024]{1,0:T(8,128)(2,1)S(1)}, bf16[768,1024]{1,0:T(8,128)(2,1)}, u32[]{:S(2)}) copy-start(bf16[768,1024]{1,0:T(8,128)(2,1)} %w_ref.3) | copy-start | bytes 4718596
  67.3 12.9 %copy-start.2 = (f32[1024]{0:T(1024)S(1)}, f32[1024]{0:T(1024)}, u32[]{:S(2)}) copy-start(f32[1024]{0:T(1024)} %param.11) | copy-start | bytes 12292
  67.3 12.9 %copy-start.3 = (f32[1024]{0:T(1024)S(1)}, f32[1024]{0:T(1024)}, u32[]{:S(2)}) copy-start(f32[1024]{0:T(1024)} %param.12) | copy-start | bytes 12292
  67.3 12.9 %copy-start.4 = (s32[128]{0:T(128)S(1)}, s32[128]{0:T(128)}, u32[]{:S(2)}) copy-start(s32[128]{0:T(128)} %param.13) | copy-start | bytes 1540
  69.5 10.7 %all-to-all-start.2 = ((bf16[4,32,1024]{2,1,0:T(8,128)(2,1)}), bf16[4,32,1024]{2,1,0:T(8,128)(2,1)S(1)}, u32[]{:S(2)}, u32[]{:S(2)}) async-start(bf16[4,32,1024]{2,1,0:T(8,128)(2,1)} %bitcast.8), calls=%async_computation.2 | async-start | bytes 524288 | tf_op jit(solution)/shard_map/all_to_all | solution.py:162

commit v2 on v1

--- a/solution.py
+++ b/solution.py
@@ -39,17 +39,17 @@
     )
 
 
-def index_kernel(rows_dev, codes_ref, cols_ref, out_ref):
+def index_kernel(rows_dev, owner_ref, offset_ref, cols_ref, out_ref):
     n_owner = out_ref.shape[0]
-    n_look = codes_ref.shape[1]
+    n_look = cols_ref.shape[1]
+    n_feat = owner_ref.shape[0]
     before = hot(iota((rows_dev, rows_dev), 0) < iota((rows_dev, rows_dev), 1))
     offsets = iota((n_owner, rows_dev), 1)
     lane = iota((n_owner, LANES), 1)
     asked = jnp.full((n_owner, LANES), -1, jnp.int32)
     for k in range(3):
-        code = codes_ref[k : k + 1, :]
-        owner = code // rows_dev
-        offset = code - owner * rows_dev
+        owner = jnp.concatenate([owner_ref[f, k : k + 1, :] for f in range(n_feat)], axis=1)
+        offset = jnp.concatenate([offset_ref[f, k : k + 1, :] for f in range(n_feat)], axis=1)
         owner_hot = hot(iota((n_owner, n_look), 0) == owner)
         offset_hot = hot(iota((rows_dev, n_look), 0) == offset)
         present = dot(owner_hot, offset_hot, 1, 1) > 0.5
@@ -103,36 +103,36 @@
     emb = (looked[0] * looked[1] + looked[2]).astype(BF16)
     n_b = n_look // n_feat
     emb = jnp.concatenate([emb[:, f * n_b : (f + 1) * n_b] for f in range(n_feat)], axis=0)
-    pre_ref[...] = dot(emb, w_ref[...], 0, 0).astype(BF16)
-
-
-def head_kernel(grp_ref, pre_ref, b_ref, w_out_ref, labels_ref, grad_ref, loss_ref):
-    n_grp, share, _ = grad_ref.shape
+    pre = dot(emb, w_ref[...], 0, 0).astype(BF16)
+    for g in range(pre_ref.shape[0]):
+        pre_ref[g] = pre
+
+
+def backward_kernel(
+    grp_ref, pre_ref, b_ref, w_out_ref, labels_ref, w_ref, cols_ref, looked_ref, out_ref, loss_ref
+):
+    n_grp, n_b, _ = pre_ref.shape
     pre = b_ref[...]
     for g in range(n_grp):
-        pre = pre + pre_ref[g * share : (g + 1) * share, :].astype(F32)
+        pre = pre + pre_ref[g].astype(F32)
     w_out = w_out_ref[...]
     sig = jax.nn.sigmoid(pre)
     logits = jnp.sum(pre * sig * w_out, axis=1, keepdims=True)
-    n_b = labels_ref.shape[1]
-    mine = iota((share, n_b), 1) == iota((share, n_b), 0) + grp_ref[0] * share
-    targets = jnp.sum(jnp.where(mine, labels_ref[...].astype(F32), 0.0), axis=1, keepdims=True)
+    diagonal = iota((n_b, n_b), 0) == iota((n_b, n_b), 1)
+    targets = jnp.sum(jnp.where(diagonal, labels_ref[...].astype(F32), 0.0), axis=1, keepdims=True)
     soft = jnp.maximum(logits, 0.0) + jnp.log1p(jnp.exp(-jnp.abs(logits)))
     losses = soft - targets * logits
+    share = loss_ref.shape[1]
+    mine = iota((n_b, share), 0) == iota((n_b, share), 1) + grp_ref[0] * share
+    loss_ref[...] = jnp.sum(jnp.where(mine, losses, 0.0), axis=0, keepdims=True)
     grad_logit = jax.nn.sigmoid(logits) - targets
     grad = (grad_logit * w_out * (sig * (1.0 + pre * (1.0 - sig)))).astype(BF16)
-    for g in range(n_grp):
-        grad_ref[g] = grad
-    diagonal = iota((share, share), 0) == iota((share, share), 1)
-    loss_ref[...] = jnp.sum(jnp.where(diagonal, losses, 0.0), axis=0, keepdims=True)
-
-
-def backward_kernel(grad_ref, w_ref, cols_ref, looked_ref, out_ref):
+
     width = out_ref.shape[1]
     n_look = cols_ref.shape[1]
     n_owner = out_ref.shape[0] // (3 * SLOTS)
     n_feat = w_ref.shape[0] // width
-    grad_t = dot(w_ref[...], grad_ref[...], 1, 1)
+    grad_t = dot(w_ref[...], grad, 1, 1)
     emb_t = jnp.concatenate([grad_t[f * width : (f + 1) * width] for f in range(n_feat)], axis=1)
     factors = (looked_ref[1].astype(F32), looked_ref[0].astype(F32), None)
     parts = []
@@ -170,31 +170,36 @@
     hidden = w_first.shape[1]
     n_look = n_b * n_feat
     shape = jax.ShapeDtypeStruct
-    codes = (owner * rows_dev + offset).transpose(2, 1, 0).reshape(3, n_look)
     cols, asked = call(
         functools.partial(index_kernel, rows_dev),
         (shape((3, n_look), jnp.int32), shape((n_rows, LANES), jnp.int32)),
-    )(codes)
+        n_in=2,
+    )(owner.transpose(1, 2, 0), offset.transpose(1, 2, 0))
     requests = exchange(asked, "rows")
     rows = call(fetch_kernel, shape((n_rows * 3 * SLOTS, width), BF16), n_in=2)(requests, tables)
     rows = exchange(rows, "rows")
     pre, looked = call(
         forward_kernel,
-        (shape((n_b, hidden), BF16), shape((2, width, n_look), BF16)),
+        (shape((n_grp, n_b, hidden), BF16), shape((2, width, n_look), BF16)),
         n_in=3,
     )(rows, cols, w_first)
     pre = exchange(pre, "grp")
     grp = lax.axis_index("grp").astype(jnp.int32).reshape(1)
     share = n_b // n_grp
-    grad, losses = call(
-        head_kernel,
-        (shape((n_grp, share, hidden), BF16), shape((1, share), F32)),
-        n_in=5,
+    sums, losses = call(
+        backward_kernel,
+        (shape((n_rows * 3 * SLOTS, width), BF16), shape((1, share), F32)),
+        n_in=8,
         scalars=(0,),
-    )(grp, pre, b_first.reshape(1, hidden), w_out.reshape(1, hidden), labels.reshape(1, n_b))
-    grad = exchange(grad.reshape(n_b, hidden), "grp")
-    sums = call(backward_kernel, shape((n_rows * 3 * SLOTS, width), BF16), n_in=4)(
-        grad, w_first, cols, looked
+    )(
+        grp,
+        pre,
+        b_first.reshape(1, hidden),
+        w_out.reshape(1, hidden),
+        labels.reshape(1, n_b),
+        w_first,
+        cols,
+        looked,
     )
     sums = exchange(sums, "rows")
     table_grad = call(owner_kernel, shape((3, rows_dev, width), F32), n_in=2)(requests, sums)

time: 127 us -> 128 us (level)
  blocking collectives: 102 us -> 92.7 us
  waiting for transfers between devices: 6.67 us -> 15.1 us
  local copies, waits for them, and re-layouts: 1.15 us -> 3.52 us
    all_to_all x4 -> x3, blocking collectives: 102 us -> 92.7 us  [exchange(): return lax.all_to_all(array, axis, split_axis=0, concat_axis=0, tiled=True)]
    all_to_all x1, waiting for transfers between devices: 6.67 us -> 15.1 us  [exchange(): return lax.all_to_all(array, axis, split_axis=0, concat_axis=0, tiled=True)]
    unnamed x10 -> x16, local copies, waits for them, and re-layouts: 1.15 us -> 3.52 us
    pallas_call x3 -> x2, Pallas kernels: 5.52 us -> 4.41 us  [the longest x1 2.92 us: body(): call(backward_kernel, (shape((n_rows * 3 * SLOTS, width), BF16), shape((1...]
where the time goes in v2:
time: 128 us; the launch traced here: 127 us
  blocking collectives  92.7 us (72%)
  waiting for transfers between devices  15.1 us (12%)
  Pallas kernels  11.1 us (9%)
  starting transfers between devices  4.15 us (3%)
  local copies, waits for them, and re-layouts  3.52 us (3%)
    all_to_all x3, blocking collectives, exchange(): return lax.all_to_all(array, axis, split_axis=0, concat_axis=0, tiled=True)  92.7 us
    all_to_all x1, waiting for transfers between devices, exchange(): return lax.all_to_all(array, axis, split_axis=0, concat_axis=0, tiled=True)  15.1 us
    all_to_all x1, starting transfers between devices, exchange(): return lax.all_to_all(array, axis, split_axis=0, concat_axis=0, tiled=True)  4.15 us
    unnamed x16, local copies, waits for them, and re-layouts  3.52 us
    pallas_call x1, Pallas kernels, body(): call(backward_kernel, (shape((n_rows * 3 * SLOTS, width), BF16), shape((1...  2.92 us
    pallas_call x1, Pallas kernels, body(): call(owner_kernel, shape((3, rows_dev, width), F32), n_in=2)(requests, sums)  2.7 us
    pallas_call x1, Pallas kernels, body(): call(functools.partial(index_kernel, rows_dev), (shape((3, n_look), jnp.i...  2.68 us
  transfers between devices with their start and end apart: 1, of which 1 were waited for; matrix products, arithmetic and copies ran while one was open for 0% of the time, Pallas kernels for 0%

profile of v2, /device:TPU:1, one launch (start us, length us, event | category | flops | bytes accessed | tf_op | source)
XLA Modules:
  0.0 127.2 jit_solution(18079335069003278592)
XLA Ops:
  0.6 0.0 copy-start.3
  0.6 0.7 copy-done.3
  1.3 0.0 copy-start.4
  1.3 0.7 copy-done.4
  2.0 2.7 %shard_map.86 = (s32[3,768]{1,0:T(4,128)S(1)}, s32[128,128]{1,0:T(8,128)S(1)}) custom-call(s32[6,3,128]{2,1,0:T(4,128)S(1)} %bitcast.22, s32[6,3,128]{2,1,0:T(4,128)S(1)} %bitcast.23), custom_call_target="tpu_custom_call" | custom-call | bytes 1048576 | tf_op jit(solution)/shard_map/pallas_call | solution.py:173
  4.7 29.7 %all_to_all.38 = s32[128,1,128]{2,1,0:T(1,128)S(1)} all-to-all(s32[128,1,128]{2,1,0:T(1,128)S(1)} %bitcast.21), channel_id=1, replica_groups=mesh['rows'=128,'grp'=4] {'rows'}, dimensions={0} | all-to-all | bytes 131072 | tf_op jit(solution)/shard_map/all_to_all | solution.py:162
  34.4 0.0 copy-start.2
  34.4 1.1 copy-done.2
  35.5 0.0 copy-start
  35.5 1.3 %shard_map.87 = bf16[3072,128]{1,0:T(8,128)(2,1)S(1)} custom-call(s32[128,128]{1,0:T(8,128)S(1)} %bitcast.19, f32[3,512,128]{2,1,0:T(8,128)S(1)} %copy-done.2), custom_call_target="tpu_custom_call" | custom-call | bytes 1048576 | tf_op jit(solution)/shard_map/pallas_call | solution.py:179
  36.8 31.1 %all_to_all.39 = bf16[128,24,128]{2,1,0:T(8,128)(2,1)S(1)} all-to-all(bf16[128,24,128]{2,1,0:T(8,128)(2,1)S(1)} %bitcast.16), channel_id=1, replica_groups=mesh['rows'=128,'grp'=4] {'rows'}, dimensions={0} | all-to-all | bytes 1572864 | tf_op jit(solution)/shard_map/all_to_all | solution.py:162
  68.0 0.0 copy-done
  68.0 1.5 %shard_map.88 = (bf16[4,128,1024]{2,1,0:T(8,128)(2,1)S(1)}, bf16[2,128,768]{2,1,0:T(8,128)(2,1)S(1)}) custom-call(bf16[3072,128]{1,0:T(8,128)(2,1)S(1)} %bitcast.17, s32[3,768]{1,0:T(4,128)S(1)} %get-tuple-element.9.cols_ref, bf16[768,1024]{1,0:T(8,128)(2,1)S(1)} %copy-done), custom_call_target="tpu_custom_call" | custom-call | bytes 1048576 | tf_op jit(solution)/shard_map/pallas_call | solution.py:181
  69.5 0.0 copy-start.1
  69.5 1.0 copy-done.1
  70.4 0.0 copy-start.5
  70.4 0.0 copy-start.6
  70.4 0.0 copy-start.7
  70.4 4.1 %all-to-all-start.2 = ((bf16[4,128,1024]{2,1,0:T(8,128)(2,1)}), bf16[4,128,1024]{2,1,0:T(8,128)(2,1)S(1)}, u32[]{:S(2)}, u32[]{:S(2)}) async-start(bf16[4,128,1024]{2,1,0:T(8,128)(2,1)} %copy-done.1), calls=%async_computation.2 | async-start | bytes 2097152 | tf_op jit(solution)/shard_map/all_to_all | solution.py:162
  74.6 15.1 %all-to-all-done.2.pre_ref = bf16[4,128,1024]{2,1,0:T(8,128)(2,1)S(1)} async-done(((bf16[4,128,1024]{2,1,0:T(8,128)(2,1)}), bf16[4,128,1024]{2,1,0:T(8,128)(2,1)S(1)}, u32[]{:S(2)}, u32[]{:S(2)}) %all-to-all-start.2) | async-done | bytes 1048608 | tf_op jit(solution)/shard_map/all_to_all | solution.py:162
  89.7 0.0 copy-done.5
  89.7 0.0 copy-done.6
  89.7 0.0 copy-done.7
  89.7 2.9 %shard_map.89 = (bf16[3072,128]{1,0:T(8,128)(2,1)S(1)}, f32[1,32]{1,0:T(1,128)}) custom-call(s32[1]{0:T(128)} %bitcast.5.grp_ref, bf16[4,128,1024]{2,1,0:T(8,128)(2,1)S(1)} %all-to-all-done.2.pre_ref, f32[1,1024]{1,0:T(1,128)S(1)} %bitcast.24, f32[1,1024]{1,0:T(1,128)S(1)} %bitcast.25, s32[1,128]{1,0:T(1,128)S(1)} %bitcast.26, ...), custom_call_target="tpu_custom_call" | custom-call | bytes 1048576 | tf_op jit(solution)/shard_map/pallas_call | solution.py:189
  92.6 31.9 %all_to_all.40 = bf16[128,24,128]{2,1,0:T(8,128)(2,1)S(1)} all-to-all(bf16[128,24,128]{2,1,0:T(8,128)(2,1)S(1)} %bitcast.18), channel_id=1, replica_groups=mesh['rows'=128,'grp'=4] {'rows'}, dimensions={0} | all-to-all | bytes 1572864 | tf_op jit(solution)/shard_map/all_to_all | solution.py:162
  124.5 2.7 %shard_map.90 = f32[3,512,128]{2,1,0:T(8,128)} custom-call(s32[128,128]{1,0:T(8,128)S(1)} %bitcast.20, bf16[3072,128]{1,0:T(8,128)(2,1)S(1)} %bitcast.15), custom_call_target="tpu_custom_call" | custom-call | bytes 1048576 | tf_op jit(solution)/shard_map/pallas_call | solution.py:205
Async XLA Ops:
  0.6 0.7 copy-start.3
  1.3 0.7 copy-start.4
  34.4 1.1 copy-start.2
  35.5 32.4 %copy-start = (bf16[768,1024]{1,0:T(8,128)(2,1)S(1)}, bf16[768,1024]{1,0:T(8,128)(2,1)}, u32[]{:S(2)}) copy-start(bf16[768,1024]{1,0:T(8,128)(2,1)} %w_ref.3) | copy-start | bytes 4718596
  69.5 1.0 copy-start.1
  70.4 19.3 %copy-start.5 = (f32[1024]{0:T(1024)S(1)}, f32[1024]{0:T(1024)}, u32[]{:S(2)}) copy-start(f32[1024]{0:T(1024)} %param.11) | copy-start | bytes 12292
  70.4 19.3 %copy-start.6 = (f32[1024]{0:T(1024)S(1)}, f32[1024]{0:T(1024)}, u32[]{:S(2)}) copy-start(f32[1024]{0:T(1024)} %param.12) | copy-start | bytes 12292
  70.4 19.3 %copy-start.7 = (s32[128]{0:T(128)S(1)}, s32[128]{0:T(128)}, u32[]{:S(2)}) copy-start(s32[128]{0:T(128)} %param.13) | copy-start | bytes 1540
  70.4 19.3 %all-to-all-start.2 = ((bf16[4,128,1024]{2,1,0:T(8,128)(2,1)}), bf16[4,128,1024]{2,1,0:T(8,128)(2,1)S(1)}, u32[]{:S(2)}, u32[]{:S(2)}) async-start(bf16[4,128,1024]{2,1,0:T(8,128)(2,1)} %copy-done.1), calls=%async_computation.2 | async-start | bytes 2097152 | tf_op jit(solution)/shard_map/all_to_all | solution.py:162

commit v3 on v2

--- a/solution.py
+++ b/solution.py
@@ -1,5 +1,3 @@
-import functools
-
 import jax
 import jax.numpy as jnp
 from jax import lax
@@ -10,6 +8,7 @@
 SLOTS = 8
 LANES = 128
 VMEM = 40 * 2**20
+VMEM_INDEX = 55_750_000
 BF16 = jnp.bfloat16
 F32 = jnp.float32
 
@@ -26,30 +25,42 @@
     return jnp.where(mask, 1.0, 0.0).astype(BF16)
 
 
-def call(kernel, out_shape, flops=0, n_in=1, scalars=()):
-    specs = [
-        pl.BlockSpec(memory_space=pltpu.SMEM if i in scalars else pltpu.VMEM) for i in range(n_in)
-    ]
+def call(kernel, out_shape, n_in=1, spaces=None, scratch=(), vmem=VMEM, flops=0):
+    spaces = spaces or [pltpu.VMEM] * n_in
     return pl.pallas_call(
         kernel,
         out_shape=out_shape,
-        in_specs=specs,
-        compiler_params=pltpu.CompilerParams(vmem_limit_bytes=VMEM),
+        in_specs=[pl.BlockSpec(memory_space=space) for space in spaces],
+        scratch_shapes=scratch,
+        compiler_params=pltpu.CompilerParams(vmem_limit_bytes=vmem),
         cost_estimate=pl.CostEstimate(flops=flops, bytes_accessed=2**20, transcendentals=0),
     )
 
 
-def index_kernel(rows_dev, owner_ref, offset_ref, cols_ref, out_ref):
+def index_kernel(
+    codes_ref,
+    table_hbm,
+    grp_ref,
+    cols_ref,
+    out_ref,
+    low_ref,
+    table_ref,
+    sem,
+):
+    copy = pltpu.make_async_copy(table_hbm, table_ref, sem)
+    copy.start()
+    rows_dev = table_ref.shape[1]
     n_owner = out_ref.shape[0]
     n_look = cols_ref.shape[1]
-    n_feat = owner_ref.shape[0]
+    n_feat = codes_ref.shape[0]
     before = hot(iota((rows_dev, rows_dev), 0) < iota((rows_dev, rows_dev), 1))
     offsets = iota((n_owner, rows_dev), 1)
     lane = iota((n_owner, LANES), 1)
     asked = jnp.full((n_owner, LANES), -1, jnp.int32)
     for k in range(3):
-        owner = jnp.concatenate([owner_ref[f, k : k + 1, :] for f in range(n_feat)], axis=1)
-        offset = jnp.concatenate([offset_ref[f, k : k + 1, :] for f in range(n_feat)], axis=1)
+        code = jnp.concatenate([codes_ref[f, k : k + 1, :] for f in range(n_feat)], axis=1)
+        owner = code // rows_dev
+        offset = code - owner * rows_dev
         owner_hot = hot(iota((n_owner, n_look), 0) == owner)
         offset_hot = hot(iota((rows_dev, n_look), 0) == offset)
         present = dot(owner_hot, offset_hot, 1, 1) > 0.5
@@ -63,6 +74,9 @@
             found = jnp.sum(found, axis=1, keepdims=True).astype(jnp.int32) - 1
             asked = jnp.where(lane == k * SLOTS + s, found, asked)
     out_ref[...] = asked
+    cols_ref[3:4, :] = jnp.full((1, n_look), grp_ref[0], jnp.int32)
+    copy.wait()
+    low_ref[...] = table_ref[...].astype(BF16)
 
 
 def request_column(codes, k):
@@ -81,7 +95,7 @@
     parts = []
     for k in range(3):
         onehot = hot(iota((n_src * SLOTS, rows_dev), 1) == request_column(codes, k))
-        rows = dot(onehot, table_ref[k].astype(BF16), 1, 0)
+        rows = dot(onehot, table_ref[k], 1, 0)
         parts.append(rows.reshape(n_src, SLOTS, width))
     rows = jnp.concatenate(parts, axis=1)
     out_ref[...] = rows.reshape(n_src * 3 * SLOTS, width).astype(BF16)
@@ -109,7 +123,7 @@
 
 
 def backward_kernel(
-    grp_ref, pre_ref, b_ref, w_out_ref, labels_ref, w_ref, cols_ref, looked_ref, out_ref, loss_ref
+    pre_ref, b_ref, w_out_ref, labels_ref, w_ref, cols_ref, looked_ref, out_ref, loss_ref
 ):
     n_grp, n_b, _ = pre_ref.shape
     pre = b_ref[...]
@@ -123,7 +137,7 @@
     soft = jnp.maximum(logits, 0.0) + jnp.log1p(jnp.exp(-jnp.abs(logits)))
     losses = soft - targets * logits
     share = loss_ref.shape[1]
-    mine = iota((n_b, share), 0) == iota((n_b, share), 1) + grp_ref[0] * share
+    mine = iota((n_b, share), 0) == iota((n_b, share), 1) + cols_ref[3:4, :share] * share
     loss_ref[...] = jnp.sum(jnp.where(mine, losses, 0.0), axis=0, keepdims=True)
     grad_logit = jax.nn.sigmoid(logits) - targets
     grad = (grad_logit * w_out * (sig * (1.0 + pre * (1.0 - sig)))).astype(BF16)
@@ -170,13 +184,26 @@
     hidden = w_first.shape[1]
     n_look = n_b * n_feat
     shape = jax.ShapeDtypeStruct
-    cols, asked = call(
-        functools.partial(index_kernel, rows_dev),
-        (shape((3, n_look), jnp.int32), shape((n_rows, LANES), jnp.int32)),
-        n_in=2,
-    )(owner.transpose(1, 2, 0), offset.transpose(1, 2, 0))
+    cols, asked, low = call(
+        index_kernel,
+        (
+            shape((4, n_look), jnp.int32),
+            shape((n_rows, LANES), jnp.int32),
+            shape(tables.shape, BF16),
+        ),
+        spaces=[pltpu.VMEM, pltpu.HBM, pltpu.SMEM],
+        vmem=VMEM_INDEX,
+        scratch=(
+            pltpu.VMEM(tables.shape, F32),
+            pltpu.SemaphoreType.DMA,
+        ),
+    )(
+        (owner * rows_dev + offset).transpose(1, 2, 0),
+        tables,
+        lax.axis_index("grp").astype(jnp.int32).reshape(1),
+    )
     requests = exchange(asked, "rows")
-    rows = call(fetch_kernel, shape((n_rows * 3 * SLOTS, width), BF16), n_in=2)(requests, tables)
+    rows = call(fetch_kernel, shape((n_rows * 3 * SLOTS, width), BF16), n_in=2)(requests, low)
     rows = exchange(rows, "rows")
     pre, looked = call(
         forward_kernel,
@@ -184,15 +211,12 @@
         n_in=3,
     )(rows, cols, w_first)
     pre = exchange(pre, "grp")
-    grp = lax.axis_index("grp").astype(jnp.int32).reshape(1)
     share = n_b // n_grp
     sums, losses = call(
         backward_kernel,
         (shape((n_rows * 3 * SLOTS, width), BF16), shape((1, share), F32)),
-        n_in=8,
-        scalars=(0,),
+        n_in=7,
     )(
-        grp,
         pre,
         b_first.reshape(1, hidden),
         w_out.reshape(1, hidden),

time: 128 us -> 125 us (0.977)
  blocking collectives: 92.7 us -> 112 us
  waiting for transfers between devices: 15.1 us -> 0 us
  starting transfers between devices: 4.15 us -> 0 us
  local copies, waits for them, and re-layouts: 3.52 us -> 0.03 us
    all_to_all x3 -> x4, blocking collectives: 92.7 us -> 112 us  [exchange(): return lax.all_to_all(array, axis, split_axis=0, concat_axis=0, tiled=True)]
    all_to_all x1 -> x0, waiting for transfers between devices: 15.1 us -> none  [exchange(): return lax.all_to_all(array, axis, split_axis=0, concat_axis=0, tiled=True)]
    all_to_all x1 -> x0, starting transfers between devices: 4.15 us -> none  [exchange(): return lax.all_to_all(array, axis, split_axis=0, concat_axis=0, tiled=True)]
    unnamed x16 -> x8, local copies, waits for them, and re-layouts: 3.52 us -> 0.03 us
  transfers between devices with their start and end apart: 1 -> 0, of which waited for: 1 -> 0; matrix products, arithmetic and copies ran while one was open for 0% -> 0% of each run, Pallas kernels for 0% -> 0%
where the time goes in v3:
time: 125 us
  blocking collectives  112 us (90%)
  Pallas kernels  11.2 us (9%)
    all_to_all x4, blocking collectives, exchange(): return lax.all_to_all(array, axis, split_axis=0, concat_axis=0, tiled=True)  112 us
    pallas_call x1, Pallas kernels, body(): call(backward_kernel, (shape((n_rows * 3 * SLOTS, width), BF16), shape((1...  2.94 us
    pallas_call x1, Pallas kernels, body(): call(index_kernel, (shape((4, n_look), jnp.int32), shape((n_rows, LANES),...  2.79 us
    pallas_call x1, Pallas kernels, body(): call(owner_kernel, shape((3, rows_dev, width), F32), n_in=2)(requests, sums)  2.7 us

profile of v3, /device:TPU:1, one launch (start us, length us, event | category | flops | bytes accessed | tf_op | source)
XLA Modules:
  0.0 124.5 jit_solution(15477929229710319678)
XLA Ops:
  0.6 0.7 add_bitcast_fusion.codes_ref
  1.4 2.8 %shard_map.86 = (s32[4,768]{1,0:T(4,128)S(1)}, s32[128,128]{1,0:T(8,128)S(1)}, bf16[3,512,128]{2,1,0:T(8,128)(2,1)S(1)}) custom-call(s32[6,3,128]{2,1,0:T(4,128)S(1)} %add_bitcast_fusion.codes_ref, f32[3,512,128]{2,1,0:T(8,128)} %table_hbm.1, s32[1]{0:T(128)} %bitcast.1.grp_ref), custom_call_target="tpu_custom_call" | custom-call | bytes 1048576 | tf_op jit(solution)/shard_map/pallas_call | solution.py:187
  4.2 0.0 copy-start
  4.2 29.8 %all_to_all.38 = s32[128,1,128]{2,1,0:T(1,128)S(1)} all-to-all(s32[128,1,128]{2,1,0:T(1,128)S(1)} %bitcast.21), channel_id=1, replica_groups=mesh['rows'=128,'grp'=4] {'rows'}, dimensions={0} | all-to-all | bytes 131072 | tf_op jit(solution)/shard_map/all_to_all | solution.py:176
  34.0 1.3 %shard_map.87 = bf16[3072,128]{1,0:T(8,128)(2,1)S(1)} custom-call(s32[128,128]{1,0:T(8,128)S(1)} %bitcast.19, bf16[3,512,128]{2,1,0:T(8,128)(2,1)S(1)} %get-tuple-element.10.table_ref), custom_call_target="tpu_custom_call" | custom-call | bytes 1048576 | tf_op jit(solution)/shard_map/pallas_call | solution.py:206
  35.3 31.1 %all_to_all.39 = bf16[128,24,128]{2,1,0:T(8,128)(2,1)S(1)} all-to-all(bf16[128,24,128]{2,1,0:T(8,128)(2,1)S(1)} %bitcast.16), channel_id=1, replica_groups=mesh['rows'=128,'grp'=4] {'rows'}, dimensions={0} | all-to-all | bytes 1572864 | tf_op jit(solution)/shard_map/all_to_all | solution.py:176
  66.4 0.0 copy-done
  66.4 1.5 %shard_map.88 = (bf16[4,128,1024]{2,1,0:T(8,128)(2,1)S(1)}, bf16[2,128,768]{2,1,0:T(8,128)(2,1)S(1)}) custom-call(bf16[3072,128]{1,0:T(8,128)(2,1)S(1)} %bitcast.17, s32[4,768]{1,0:T(4,128)S(1)} %get-tuple-element.11.cols_ref, bf16[768,1024]{1,0:T(8,128)(2,1)S(1)} %copy-done), custom_call_target="tpu_custom_call" | custom-call | bytes 1048576 | tf_op jit(solution)/shard_map/pallas_call | solution.py:208
  67.9 0.0 copy-start.1
  67.9 0.0 copy-start.2
  67.9 0.0 copy-start.3
  67.9 18.7 %all_to_all.40.pre_ref = bf16[4,128,1024]{2,1,0:T(8,128)(2,1)S(1)} all-to-all(bf16[4,128,1024]{2,1,0:T(8,128)(2,1)S(1)} %get-tuple-element.12), channel_id=1, replica_groups=mesh['rows'=128,'grp'=4] {'grp'}, dimensions={0} | all-to-all | bytes 2097152 | tf_op jit(solution)/shard_map/all_to_all | solution.py:176
  86.7 0.0 copy-done.1
  86.7 0.0 copy-done.2
  86.7 0.0 copy-done.3
  86.7 2.9 %shard_map.89 = (bf16[3072,128]{1,0:T(8,128)(2,1)S(1)}, f32[1,32]{1,0:T(1,128)}) custom-call(bf16[4,128,1024]{2,1,0:T(8,128)(2,1)S(1)} %all_to_all.40.pre_ref, f32[1,1024]{1,0:T(1,128)S(1)} %bitcast.22, f32[1,1024]{1,0:T(1,128)S(1)} %bitcast.23, s32[1,128]{1,0:T(1,128)S(1)} %bitcast.24, bf16[768,1024]{1,0:T(8,128)(2,1)S(1)} %copy-done, ...), custom_call_target="tpu_custom_call" | custom-call | bytes 1048576 | tf_op jit(solution)/shard_map/pallas_call | solution.py:215
  89.7 32.2 %all_to_all.41 = bf16[128,24,128]{2,1,0:T(8,128)(2,1)S(1)} all-to-all(bf16[128,24,128]{2,1,0:T(8,128)(2,1)S(1)} %bitcast.18), channel_id=1, replica_groups=mesh['rows'=128,'grp'=4] {'rows'}, dimensions={0} | all-to-all | bytes 1572864 | tf_op jit(solution)/shard_map/all_to_all | solution.py:176
  121.8 2.7 %shard_map.90 = f32[3,512,128]{2,1,0:T(8,128)} custom-call(s32[128,128]{1,0:T(8,128)S(1)} %bitcast.20, bf16[3072,128]{1,0:T(8,128)(2,1)S(1)} %bitcast.15), custom_call_target="tpu_custom_call" | custom-call | bytes 1048576 | tf_op jit(solution)/shard_map/pallas_call | solution.py:229
Async XLA Ops:
  4.2 62.3 %copy-start = (bf16[768,1024]{1,0:T(8,128)(2,1)S(1)}, bf16[768,1024]{1,0:T(8,128)(2,1)}, u32[]{:S(2)}) copy-start(bf16[768,1024]{1,0:T(8,128)(2,1)} %w_ref.3) | copy-start | bytes 4718596
  67.9 18.8 %copy-start.1 = (f32[1024]{0:T(1024)S(1)}, f32[1024]{0:T(1024)}, u32[]{:S(2)}) copy-start(f32[1024]{0:T(1024)} %param.11) | copy-start | bytes 12292
  67.9 18.8 %copy-start.2 = (f32[1024]{0:T(1024)S(1)}, f32[1024]{0:T(1024)}, u32[]{:S(2)}) copy-start(f32[1024]{0:T(1024)} %param.12) | copy-start | bytes 12292
  67.9 18.8 %copy-start.3 = (s32[128]{0:T(128)S(1)}, s32[128]{0:T(128)}, u32[]{:S(2)}) copy-start(s32[128]{0:T(128)} %param.13) | copy-start | bytes 1540

commit v4 on v3

v4 whole, which is shorter than its diff:
```python
import jax
import jax.numpy as jnp
from jax import lax
from jax.experimental import pallas as pl
from jax.experimental.pallas import tpu as pltpu
from jax.sharding import PartitionSpec as P

SLOTS = 8
LANES = 128
VMEM = 40 * 2**20
BF16 = jnp.bfloat16
F32 = jnp.float32


def dot(a, b, ca, cb):
    return lax.dot_general(a, b, (((ca,), (cb,)), ((), ())), preferred_element_type=F32)


def iota(shape, dim):
    return lax.broadcasted_iota(jnp.int32, shape, dim)


def one_hot(size, index):
    shape = (size, index.shape[1])
    same = lax.broadcasted_iota(jnp.int16, shape, 0) == index.astype(jnp.int16)
    return jnp.where(same, jnp.ones((), BF16), jnp.zeros((), BF16))


def call(kernel, out_shape, n_in=1, spaces=None, out=None, scratch=()):
    spaces = spaces or [pltpu.VMEM] * n_in
    return pl.pallas_call(
        kernel,
        out_shape=out_shape,
        in_specs=[pl.BlockSpec(memory_space=space) for space in spaces],
        scratch_shapes=scratch,
        **({} if out is None else {"out_specs": pl.BlockSpec(memory_space=out)}),
        compiler_params=pltpu.CompilerParams(vmem_limit_bytes=VMEM),
        cost_estimate=pl.CostEstimate(flops=2**28, bytes_accessed=2**20, transcendentals=0),
    )


def index_kernel(
    owner_hbm,
    offset_hbm,
    table_hbm,
    grp_ref,
    cols_ref,
    out_ref,
    table_ref,
    owner_ref,
    offset_ref,
    sems,
):
    copies = [
        pltpu.make_async_copy(owner_hbm, owner_ref, sems.at[0]),
        pltpu.make_async_copy(offset_hbm, offset_ref, sems.at[1]),
        pltpu.make_async_copy(table_hbm, table_ref, sems.at[2]),
    ]
    for copy in copies:
        copy.start()
    rows_dev = table_ref.shape[1]
    n_owner = out_ref.shape[0]
    n_look = cols_ref.shape[1]
    n_feat = owner_ref.shape[0]
    shape = (rows_dev, rows_dev)
    before = jnp.where(iota(shape, 1) < iota(shape, 0), 1.0, 0.0).astype(BF16)
    pairs = []
    copies[0].wait()
    copies[1].wait()
    for k in range(3):
        owner = jnp.concatenate([owner_ref[f, k : k + 1, :] for f in range(n_feat)], axis=1)
        offset = jnp.concatenate([offset_ref[f, k : k + 1, :] for f in range(n_feat)], axis=1)
        pairs.append((owner, offset, one_hot(n_owner, owner), one_hot(rows_dev, offset)))
    by_look = [owner_hot.T for _, _, owner_hot, _ in pairs]
    present = jnp.concatenate([dot(pairs[k][3], by_look[k], 1, 0) for k in range(3)], axis=1)
    rank = dot(before, jnp.minimum(present, 1.0).astype(BF16), 1, 0).astype(BF16)
    asked = []
    for k in range(3):
        owner, offset, owner_hot, offset_hot = pairs[k]
        at_owner = dot(rank[:, k * n_owner : (k + 1) * n_owner], offset_hot, 0, 0)
        slot = jnp.sum(owner_hot.astype(F32) * at_owner, axis=0, keepdims=True).astype(jnp.int32)
        cols_ref[k : k + 1, :] = owner * SLOTS + slot
        slot_hot = jnp.where(iota((SLOTS, n_look), 0) == slot, 1.0, 0.0)
        high = offset // 16
        low = (offset - high * 16).astype(F32)
        sides = [slot_hot * high.astype(F32), slot_hot * low, slot_hot]
        sums = dot(jnp.concatenate(sides, axis=0).astype(BF16), by_look[k], 1, 0)
        high, low, count = (sums[i * SLOTS : (i + 1) * SLOTS] for i in range(3))
        offset = jnp.floor((high * 16.0 + low) / jnp.maximum(count, 1.0) + 0.5)
        asked.append(jnp.where(count > 0.5, offset, -1.0))
    asked.append(jnp.full((LANES - 3 * SLOTS, n_owner), -1.0, F32))
    out_ref[...] = jnp.concatenate(asked, axis=0).T.astype(jnp.int32)
    cols_ref[3:4, :] = jnp.full((1, n_look), grp_ref[0], jnp.int32)
    copies[2].wait()


def fetch_kernel(codes_ref, table_ref, out_ref, asked_ref):
    n_src = codes_ref.shape[0]
    rows_dev, width = table_ref.shape[1:]
    n_ask = n_src * SLOTS
    code = codes_ref[...] + 1
    high = code // 16
    low = (code - high * 16).astype(F32).astype(BF16)
    high = high.astype(F32).astype(BF16)
    spread = one_hot(n_src, iota((1, n_ask), 1) // SLOTS)
    wide = dot(high, spread, 0, 0) * 16.0 + dot(low, spread, 0, 0)
    mine = iota((SLOTS, n_ask), 0) == iota((SLOTS, n_ask), 1) % SLOTS
    parts = []
    for k in range(3):
        asked = jnp.where(mine, wide[k * SLOTS : (k + 1) * SLOTS], 0.0)
        asked = jnp.sum(asked, axis=0, keepdims=True).astype(jnp.int32) - 1
        asked_ref[k : k + 1, :] = asked
        rows = dot(table_ref[k].astype(BF16), one_hot(rows_dev, asked), 0, 0).T
        parts.append(rows.reshape(n_src, SLOTS, width))
    rows = jnp.concatenate(parts, axis=1)
    out_ref[...] = rows.reshape(n_ask * 3, width).astype(BF16)


def forward_kernel(rows_ref, cols_ref, w_ref, pre_ref, looked_ref):
    width = rows_ref.shape[1]
    n_look = cols_ref.shape[1]
    n_owner = rows_ref.shape[0] // (3 * SLOTS)
    n_feat = w_ref.shape[0] // width
    rows = rows_ref[...].astype(F32).reshape(n_owner, 3 * SLOTS, width)
    looked = []
    for k in range(3):
        mine = rows[:, k * SLOTS : (k + 1) * SLOTS, :].reshape(n_owner * SLOTS, width).astype(BF16)
        onehot = one_hot(n_owner * SLOTS, cols_ref[k : k + 1, :])
        looked.append(dot(mine, onehot, 0, 0))
    looked_ref[0] = looked[0].T.astype(BF16)
    looked_ref[1] = looked[1].T.astype(BF16)
    emb = (looked[0] * looked[1] + looked[2]).astype(BF16)
    n_b = n_look // n_feat
    emb = jnp.concatenate([emb[:, f * n_b : (f + 1) * n_b] for f in range(n_feat)], axis=0)
    pre = dot(emb, w_ref[...], 0, 0).astype(BF16)
    for g in range(pre_ref.shape[0]):
        pre_ref[g] = pre


def backward_kernel(
    pre_ref, b_ref, w_out_ref, labels_ref, w_ref, cols_ref, looked_ref, out_ref, loss_ref
):
    n_grp, n_b, _ = pre_ref.shape
    pre = b_ref[...]
    for g in range(n_grp):
        pre = pre + pre_ref[g].astype(F32)
    w_out = w_out_ref[...]
    sig = jax.nn.sigmoid(pre)
    logits = jnp.sum(pre * sig * w_out, axis=1, keepdims=True)
    diagonal = iota((n_b, n_b), 0) == iota((n_b, n_b), 1)
    targets = jnp.sum(jnp.where(diagonal, labels_ref[...].astype(F32), 0.0), axis=1, keepdims=True)
    soft = jnp.maximum(logits, 0.0) + jnp.log1p(jnp.exp(-jnp.abs(logits)))
    losses = soft - targets * logits
    share = loss_ref.shape[1]
    mine = iota((n_b, share), 0) == iota((n_b, share), 1) + cols_ref[3:4, :share] * share
    loss_ref[...] = jnp.sum(jnp.where(mine, losses, 0.0), axis=0, keepdims=True)
    grad_logit = jax.nn.sigmoid(logits) - targets
    grad = (grad_logit * w_out * (sig * (1.0 + pre * (1.0 - sig)))).astype(BF16)

    width = out_ref.shape[1]
    n_look = cols_ref.shape[1]
    n_owner = out_ref.shape[0] // (3 * SLOTS)
    n_feat = w_ref.shape[0] // width
    grad_emb = dot(grad, w_ref[...], 1, 1)
    emb_t = jnp.concatenate([grad_emb[:, f * width : (f + 1) * width] for f in range(n_feat)], axis=0)
    factors = (looked_ref[1].astype(F32), looked_ref[0].astype(F32), None)
    parts = []
    for k in range(3):
        row_t = emb_t if factors[k] is None else emb_t * factors[k]
        high = row_t.astype(BF16)
        low = (row_t - high.astype(F32)).astype(BF16)
        onehot = one_hot(n_owner * SLOTS, cols_ref[k : k + 1, :])
        sums = dot(onehot, jnp.concatenate([high, low], axis=1), 1, 0)
        sums = sums[:, :width] + sums[:, width:]
        parts.append(sums.reshape(n_owner, SLOTS, width))
    out_ref[...] = jnp.concatenate(parts, axis=1).reshape(n_owner * 3 * SLOTS, width).astype(BF16)


def owner_kernel(asked_ref, grads_ref, out_hbm, out_ref, sems):
    n_ask = asked_ref.shape[1]
    rows_dev, width = out_ref.shape[1:]
    grads = grads_ref[...].astype(F32).reshape(n_ask // SLOTS, 3 * SLOTS, width)
    copies = []
    for k in range(3):
        mine = grads[:, k * SLOTS : (k + 1) * SLOTS, :].reshape(n_ask, width).astype(BF16)
        out_ref[k] = dot(one_hot(rows_dev, asked_ref[k : k + 1, :]), mine, 1, 0)
        copies.append(pltpu.make_async_copy(out_ref.at[k], out_hbm.at[k], sems.at[k]))
        copies[k].start()
    for copy in copies:
        copy.wait()


def exchange(array, axis):
    return lax.all_to_all(array, axis, split_axis=0, concat_axis=0, tiled=True)


def body(owner, offset, tables, w_first, b_first, w_out, labels):
    n_rows = lax.axis_size("rows")
    n_grp = lax.axis_size("grp")
    n_b, n_feat = owner.shape[:2]
    rows_dev, width = tables.shape[1:]
    hidden = w_first.shape[1]
    n_look = n_b * n_feat
    shape = jax.ShapeDtypeStruct
    cols, asked, low = call(
        index_kernel,
        (
            shape((4, n_look), jnp.int32),
            shape((n_rows, LANES), jnp.int32),
            shape(tables.shape, F32),
        ),
        spaces=[pltpu.HBM] * 3 + [pltpu.SMEM],
        scratch=(
            pltpu.VMEM((n_feat, 3, n_b), jnp.int32),
            pltpu.VMEM((n_feat, 3, n_b), jnp.int32),
            pltpu.SemaphoreType.DMA((3,)),
        ),
    )(
        pltpu.with_memory_space_constraint(owner.transpose(1, 2, 0), pltpu.HBM),
        pltpu.with_memory_space_constraint(offset.transpose(1, 2, 0), pltpu.HBM),
        pltpu.with_memory_space_constraint(tables, pltpu.HBM),
        lax.axis_index("grp").astype(jnp.int32).reshape(1),
    )
    requests = exchange(asked, "rows")
    rows, asked = call(
        fetch_kernel,
        (
            shape((n_rows * 3 * SLOTS, width), BF16),
            shape((3, n_rows * SLOTS), jnp.int32),
        ),
        n_in=2,
    )(requests, low)
    rows = exchange(rows, "rows")
    pre, looked = call(
        forward_kernel,
        (shape((n_grp, n_b, hidden), BF16), shape((2, n_look, width), BF16)),
        n_in=3,
    )(rows, cols, w_first)
    pre = exchange(pre, "grp")
    share = n_b // n_grp
    sums, losses = call(
        backward_kernel,
        (shape((n_rows * 3 * SLOTS, width), BF16), shape((1, share), F32)),
        n_in=7,
    )(
        pre,
        b_first.reshape(1, hidden),
        w_out.reshape(1, hidden),
        labels.reshape(1, n_b),
        w_first,
        cols,
        looked,
    )
    sums = exchange(sums, "rows")
    table_grad = call(
        owner_kernel,
        shape((3, rows_dev, width), F32),
        n_in=2,
        out=pltpu.HBM,
        scratch=(pltpu.VMEM((3, rows_dev, width), F32), pltpu.SemaphoreType.DMA((3,))),
    )(asked, sums)
    return table_grad, losses.reshape(share)


def solution(mesh):
    placed = (
        P("rows", "grp", None),
        P("rows", "grp", None),
        P("grp", "rows", None),
        P("grp", None),
        P(),
        P(),
        P("rows"),
    )
    return jax.shard_map(
        body,
        mesh=mesh,
        in_specs=placed,
        out_specs=(P("grp", "rows", None), P(("rows", "grp"))),
        check_vma=False,
    )
```

time: 125 us -> 122 us (0.976)
  Pallas kernels: 11.2 us -> 9.14 us
    pallas_call x3, Pallas kernels: 5.48 us -> 4.13 us  [the longest x1 1.8 us: body(): call(owner_kernel, shape((3, rows_dev, width), F32), n_in=2, out=pltpu.HB...]
where the time goes in v4:
time: 122 us
  blocking collectives  112 us (92%)
  Pallas kernels  9.14 us (7%)
    all_to_all x4, blocking collectives, exchange(): return lax.all_to_all(array, axis, split_axis=0, concat_axis=0, tiled=True)  112 us
    pallas_call x1, Pallas kernels, body(): call(index_kernel, (shape((4, n_look), jnp.int32), shape((n_rows, LANES),...  2.75 us

profile of v4, /device:TPU:1, one launch (start us, length us, event | category | flops | bytes accessed | tf_op | source)
XLA Modules:
  0.0 121.6 jit_solution(13418779429857633468)
XLA Ops:
  0.6 2.7 %shard_map.86 = (s32[4,768]{1,0:T(4,128)S(1)}, s32[128,128]{1,0:T(8,128)S(1)}, f32[3,512,128]{2,1,0:T(8,128)S(1)}) custom-call(s32[6,3,128]{2,1,0:T(4,128)} %bitcast.24, s32[6,3,128]{2,1,0:T(4,128)} %bitcast.25, f32[3,512,128]{2,1,0:T(8,128)} %table_hbm.1, s32[1]{0:T(128)} %bitcast.2.grp_ref), custom_call_target="tpu_custom_call" | custom-call | flops 268435456 | bytes 1048576 | tf_op jit(solution)/shard_map/pallas_call | solution.py:205
  3.4 0.0 copy-start
  3.4 29.8 %all_to_all.38 = s32[128,1,128]{2,1,0:T(1,128)S(1)} all-to-all(s32[128,1,128]{2,1,0:T(1,128)S(1)} %bitcast.19), channel_id=1, replica_groups=mesh['rows'=128,'grp'=4] {'rows'}, dimensions={0} | all-to-all | bytes 131072 | tf_op jit(solution)/shard_map/all_to_all | solution.py:194
  33.2 1.0 shard_map.87
  34.2 31.1 %all_to_all.39 = bf16[128,24,128]{2,1,0:T(8,128)(2,1)S(1)} all-to-all(bf16[128,24,128]{2,1,0:T(8,128)(2,1)S(1)} %bitcast.18), channel_id=1, replica_groups=mesh['rows'=128,'grp'=4] {'rows'}, dimensions={0} | all-to-all | bytes 1572864 | tf_op jit(solution)/shard_map/all_to_all | solution.py:194
  65.3 0.0 copy-done
  65.3 1.4 %shard_map.88 = (bf16[4,128,1024]{2,1,0:T(8,128)(2,1)S(1)}, bf16[2,768,128]{2,1,0:T(8,128)(2,1)S(1)}) custom-call(bf16[3072,128]{1,0:T(8,128)(2,1)S(1)} %bitcast.16, s32[4,768]{1,0:T(4,128)S(1)} %get-tuple-element.15.cols_ref, bf16[768,1024]{1,0:T(8,128)(2,1)S(1)} %copy-done), custom_call_target="tpu_custom_call" | custom-call | flops 268435456 | bytes 1048576 | tf_op jit(solution)/shard_map/pallas_call | solution.py:234
  66.7 0.0 copy-start.1
  66.7 0.0 copy-start.2
  66.7 0.0 copy-start.3
  66.7 18.8 %all_to_all.40.pre_ref = bf16[4,128,1024]{2,1,0:T(8,128)(2,1)S(1)} all-to-all(bf16[4,128,1024]{2,1,0:T(8,128)(2,1)S(1)} %get-tuple-element.16), channel_id=1, replica_groups=mesh['rows'=128,'grp'=4] {'grp'}, dimensions={0} | all-to-all | bytes 2097152 | tf_op jit(solution)/shard_map/all_to_all | solution.py:194
  85.5 0.0 copy-done.1
  85.5 0.0 copy-done.2
  85.5 0.0 copy-done.3
  85.5 2.3 %shard_map.89 = (bf16[3072,128]{1,0:T(8,128)(2,1)S(1)}, f32[1,32]{1,0:T(1,128)}) custom-call(bf16[4,128,1024]{2,1,0:T(8,128)(2,1)S(1)} %all_to_all.40.pre_ref, f32[1,1024]{1,0:T(1,128)S(1)} %bitcast.21, f32[1,1024]{1,0:T(1,128)S(1)} %bitcast.22, s32[1,128]{1,0:T(1,128)S(1)} %bitcast.23, bf16[768,1024]{1,0:T(8,128)(2,1)S(1)} %copy-done, ...), custom_call_target="tpu_custom_call" | custom-call | flops 268435456 | bytes 1048576 | tf_op jit(solution)/shard_map/pallas_call | solution.py:241
  87.8 32.0 %all_to_all.41 = bf16[128,24,128]{2,1,0:T(8,128)(2,1)S(1)} all-to-all(bf16[128,24,128]{2,1,0:T(8,128)(2,1)S(1)} %bitcast.17), channel_id=1, replica_groups=mesh['rows'=128,'grp'=4] {'rows'}, dimensions={0} | all-to-all | bytes 1572864 | tf_op jit(solution)/shard_map/all_to_all | solution.py:194
  119.8 1.8 %shard_map.90 = f32[3,512,128]{2,1,0:T(8,128)} custom-call(s32[3,1024]{1,0:T(4,128)S(1)} %get-tuple-element.13.asked_ref, bf16[3072,128]{1,0:T(8,128)(2,1)S(1)} %bitcast.15), custom_call_target="tpu_custom_call" | custom-call | flops 268435456 | bytes 1048576 | tf_op jit(solution)/shard_map/pallas_call | solution.py:255
Async XLA Ops:
  3.4 61.9 %copy-start = (bf16[768,1024]{1,0:T(8,128)(2,1)S(1)}, bf16[768,1024]{1,0:T(8,128)(2,1)}, u32[]{:S(2)}) copy-start(bf16[768,1024]{1,0:T(8,128)(2,1)} %w_ref.3) | copy-start | bytes 4718596
  66.7 18.8 %copy-start.1 = (f32[1024]{0:T(1024)S(1)}, f32[1024]{0:T(1024)}, u32[]{:S(2)}) copy-start(f32[1024]{0:T(1024)} %param.11) | copy-start | bytes 12292
  66.7 18.8 %copy-start.2 = (f32[1024]{0:T(1024)S(1)}, f32[1024]{0:T(1024)}, u32[]{:S(2)}) copy-start(f32[1024]{0:T(1024)} %param.12) | copy-start | bytes 12292
  66.7 18.8 %copy-start.3 = (s32[128]{0:T(128)S(1)}, s32[128]{0:T(128)}, u32[]{:S(2)}) copy-start(s32[128]{0:T(128)} %param.13) | copy-start | bytes 1540

commit v5 on v4

--- a/solution.py
+++ b/solution.py
@@ -44,8 +44,9 @@
     offset_hbm,
     table_hbm,
     grp_ref,
-    cols_ref,
     out_ref,
+    keys_ref,
+    rank_ref,
     table_ref,
     owner_ref,
     offset_ref,
@@ -60,7 +61,7 @@
         copy.start()
     rows_dev = table_ref.shape[1]
     n_owner = out_ref.shape[0]
-    n_look = cols_ref.shape[1]
+    n_look = keys_ref.shape[1]
     n_feat = owner_ref.shape[0]
     shape = (rows_dev, rows_dev)
     before = jnp.where(iota(shape, 1) < iota(shape, 0), 1.0, 0.0).astype(BF16)
@@ -74,24 +75,39 @@
     by_look = [owner_hot.T for _, _, owner_hot, _ in pairs]
     present = jnp.concatenate([dot(pairs[k][3], by_look[k], 1, 0) for k in range(3)], axis=1)
     rank = dot(before, jnp.minimum(present, 1.0).astype(BF16), 1, 0).astype(BF16)
+    rank_ref[...] = rank
     asked = []
-    for k in range(3):
-        owner, offset, owner_hot, offset_hot = pairs[k]
-        at_owner = dot(rank[:, k * n_owner : (k + 1) * n_owner], offset_hot, 0, 0)
-        slot = jnp.sum(owner_hot.astype(F32) * at_owner, axis=0, keepdims=True).astype(jnp.int32)
-        cols_ref[k : k + 1, :] = owner * SLOTS + slot
-        slot_hot = jnp.where(iota((SLOTS, n_look), 0) == slot, 1.0, 0.0)
-        high = offset // 16
-        low = (offset - high * 16).astype(F32)
-        sides = [slot_hot * high.astype(F32), slot_hot * low, slot_hot]
-        sums = dot(jnp.concatenate(sides, axis=0).astype(BF16), by_look[k], 1, 0)
-        high, low, count = (sums[i * SLOTS : (i + 1) * SLOTS] for i in range(3))
-        offset = jnp.floor((high * 16.0 + low) / jnp.maximum(count, 1.0) + 0.5)
-        asked.append(jnp.where(count > 0.5, offset, -1.0))
+    numbers = lax.broadcasted_iota(jnp.int16, (rows_dev, n_owner), 0) + jnp.int16(1)
+    for k in range(3):
+        keys_ref[k : k + 1, :] = pairs[k][0]
+        keys_ref[k + 3 : k + 4, :] = pairs[k][1]
+        mine = slice(k * n_owner, (k + 1) * n_owner)
+        place = jnp.where(present[:, mine] > 0.5, rank[:, mine].astype(F32), -1.0)
+        place = place.astype(jnp.int32).astype(jnp.int16)
+        for s in range(SLOTS):
+            found = jnp.where(place == jnp.int16(s), numbers, jnp.int16(0))
+            while found.shape[0] > 16:
+                half = found.shape[0] // 2
+                found = found[:half] + found[half:]
+            found = jnp.sum(found.astype(jnp.int32).astype(F32), axis=0, keepdims=True)
+            asked.append(found - 1.0)
     asked.append(jnp.full((LANES - 3 * SLOTS, n_owner), -1.0, F32))
     out_ref[...] = jnp.concatenate(asked, axis=0).T.astype(jnp.int32)
-    cols_ref[3:4, :] = jnp.full((1, n_look), grp_ref[0], jnp.int32)
+    keys_ref[6:7, :] = jnp.full((1, n_look), grp_ref[0], jnp.int32)
     copies[2].wait()
+
+
+def prepare_kernel(keys_ref, rank_ref, w_ref, cols_ref, wt_ref):
+    rows_dev = rank_ref.shape[0]
+    n_owner = rank_ref.shape[1] // 3
+    for k in range(3):
+        owner = keys_ref[k : k + 1, :]
+        offset_hot = one_hot(rows_dev, keys_ref[k + 3 : k + 4, :])
+        at_owner = dot(rank_ref[:, k * n_owner : (k + 1) * n_owner], offset_hot, 0, 0)
+        slot = jnp.sum(one_hot(n_owner, owner).astype(F32) * at_owner, axis=0, keepdims=True)
+        cols_ref[k : k + 1, :] = owner * SLOTS + slot.astype(jnp.int32)
+    cols_ref[3:4, :] = keys_ref[6:7, :]
+    wt_ref[...] = w_ref[...].T
 
 
 def fetch_kernel(codes_ref, table_ref, out_ref, asked_ref):
@@ -160,8 +176,8 @@
     width = out_ref.shape[1]
     n_look = cols_ref.shape[1]
     n_owner = out_ref.shape[0] // (3 * SLOTS)
-    n_feat = w_ref.shape[0] // width
-    grad_emb = dot(grad, w_ref[...], 1, 1)
+    n_feat = w_ref.shape[1] // width
+    grad_emb = dot(grad, w_ref[...], 1, 0)
     emb_t = jnp.concatenate([grad_emb[:, f * width : (f + 1) * width] for f in range(n_feat)], axis=0)
     factors = (looked_ref[1].astype(F32), looked_ref[0].astype(F32), None)
     parts = []
@@ -183,9 +199,11 @@
     copies = []
     for k in range(3):
         mine = grads[:, k * SLOTS : (k + 1) * SLOTS, :].reshape(n_ask, width).astype(BF16)
-        out_ref[k] = dot(one_hot(rows_dev, asked_ref[k : k + 1, :]), mine, 1, 0)
-        copies.append(pltpu.make_async_copy(out_ref.at[k], out_hbm.at[k], sems.at[k]))
-        copies[k].start()
+        for h in range(2):
+            half = pl.ds(h * rows_dev // 2, rows_dev // 2)
+            out_ref[k, half] = dot(one_hot(rows_dev // 2, asked_ref[k : k + 1, :] - h * rows_dev // 2), mine, 1, 0)
+            copies.append(pltpu.make_async_copy(out_ref.at[k, half], out_hbm.at[k, half], sems.at[2 * k + h]))
+            copies[-1].start()
     for copy in copies:
         copy.wait()
 
@@ -202,11 +220,12 @@
     hidden = w_first.shape[1]
     n_look = n_b * n_feat
     shape = jax.ShapeDtypeStruct
-    cols, asked, low = call(
+    asked, keys, rank, table = call(
         index_kernel,
         (
-            shape((4, n_look), jnp.int32),
             shape((n_rows, LANES), jnp.int32),
+            shape((7, n_look), jnp.int32),
+            shape((rows_dev, 3 * n_rows), BF16),
             shape(tables.shape, F32),
         ),
         spaces=[pltpu.HBM] * 3 + [pltpu.SMEM],
@@ -221,6 +240,11 @@
         pltpu.with_memory_space_constraint(tables, pltpu.HBM),
         lax.axis_index("grp").astype(jnp.int32).reshape(1),
     )
+    cols, w_turned = call(
+        prepare_kernel,
+        (shape((4, n_look), jnp.int32), shape((hidden, n_feat * width), BF16)),
+        n_in=3,
+    )(keys, rank, w_first)
     requests = exchange(asked, "rows")
     rows, asked = call(
         fetch_kernel,
@@ -229,7 +253,7 @@
             shape((3, n_rows * SLOTS), jnp.int32),
         ),
         n_in=2,
-    )(requests, low)
+    )(requests, table)
     rows = exchange(rows, "rows")
     pre, looked = call(
         forward_kernel,
@@ -247,7 +271,7 @@
         b_first.reshape(1, hidden),
         w_out.reshape(1, hidden),
         labels.reshape(1, n_b),
-        w_first,
+        w_turned,
         cols,
         looked,
     )
@@ -257,7 +281,7 @@
         shape((3, rows_dev, width), F32),
         n_in=2,
         out=pltpu.HBM,
-        scratch=(pltpu.VMEM((3, rows_dev, width), F32), pltpu.SemaphoreType.DMA((3,))),
+        scratch=(pltpu.VMEM((3, rows_dev, width), F32), pltpu.SemaphoreType.DMA((6,))),
     )(asked, sums)
     return table_grad, losses.reshape(share)
 

time: 122 us -> 123 us (level)
  blocking collectives: 112 us -> 80.6 us
  waiting for transfers between devices: 0 us -> 24.2 us
  starting transfers between devices: 0 us -> 5.75 us
    all_to_all x4 -> x3, blocking collectives: 112 us -> 80.6 us  [exchange(): return lax.all_to_all(array, axis, split_axis=0, concat_axis=0, tiled=True)]
    all_to_all x0 -> x1, waiting for transfers between devices: none -> 24.2 us  [exchange(): return lax.all_to_all(array, axis, split_axis=0, concat_axis=0, tiled=True)]
    all_to_all x0 -> x1, starting transfers between devices: none -> 5.75 us  [exchange(): return lax.all_to_all(array, axis, split_axis=0, concat_axis=0, tiled=True)]
    pallas_call x1 -> x2, Pallas kernels: 2.75 us -> 2.97 us  [the longest x1 2.33 us: body(): call(index_kernel, (shape((n_rows, LANES), jnp.int32), shape((7, n_look),...]
  transfers between devices with their start and end apart: 0 -> 1, of which waited for: 0 -> 1; matrix products, arithmetic and copies ran while one was open for 0% -> 0% of each run, Pallas kernels for 0% -> 1%
where the time goes in v5:
time: 123 us; the launch traced here: 122 us
  blocking collectives  80.6 us (66%)
  waiting for transfers between devices  24.2 us (20%)
  Pallas kernels  9.9 us (8%)
  starting transfers between devices  5.75 us (5%)
    all_to_all x3, blocking collectives, exchange(): return lax.all_to_all(array, axis, split_axis=0, concat_axis=0, tiled=True)  80.6 us
    all_to_all x1, waiting for transfers between devices, exchange(): return lax.all_to_all(array, axis, split_axis=0, concat_axis=0, tiled=True)  24.2 us
    all_to_all x1, starting transfers between devices, exchange(): return lax.all_to_all(array, axis, split_axis=0, concat_axis=0, tiled=True)  5.75 us
  transfers between devices with their start and end apart: 1, of which 1 were waited for; matrix products, arithmetic and copies ran while one was open for 0% of the time, Pallas kernels for 1%

profile of v5, /device:TPU:1, one launch (start us, length us, event | category | flops | bytes accessed | tf_op | source)
XLA Modules:
  0.0 122.4 jit_solution(17728543293585488807)
XLA Ops:
  0.6 2.3 %shard_map.86 = (s32[128,128]{1,0:T(8,128)S(1)}, s32[7,768]{1,0:T(8,128)S(1)}, bf16[512,384]{1,0:T(8,128)(2,1)S(1)}, f32[3,512,128]{2,1,0:T(8,128)S(1)}) custom-call(s32[6,3,128]{2,1,0:T(4,128)} %bitcast.23, s32[6,3,128]{2,1,0:T(4,128)} %bitcast.24, f32[3,512,128]{2,1,0:T(8,128)} %table_hbm.1, s32[1]{0:T(128)} %bitcast.2.grp_ref), custom_call_target="tpu_custom_call" | custom-call | flops 268435456 | bytes 1048576 | tf_op jit(solution)/shard_map/pallas_call | solution.py:223
  3.0 0.0 copy-start
  3.0 29.8 %all_to_all.38 = s32[128,1,128]{2,1,0:T(1,128)S(1)} all-to-all(s32[128,1,128]{2,1,0:T(1,128)S(1)} %bitcast.18), channel_id=1, replica_groups=mesh['rows'=128,'grp'=4] {'rows'}, dimensions={0} | all-to-all | bytes 131072 | tf_op jit(solution)/shard_map/all_to_all | solution.py:212
  32.8 1.9 %shard_map.87 = (bf16[3072,128]{1,0:T(8,128)(2,1)}, s32[3,1024]{1,0:T(4,128)S(1)}) custom-call(s32[128,128]{1,0:T(8,128)S(1)} %bitcast.19, f32[3,512,128]{2,1,0:T(8,128)S(1)} %get-tuple-element.15.table_ref), custom_call_target="tpu_custom_call" | custom-call | flops 268435456 | bytes 1048576 | tf_op jit(solution)/shard_map/pallas_call | solution.py:249
  34.6 5.8 %all-to-all-start.1 = ((bf16[128,24,128]{2,1,0:T(8,128)(2,1)}), bf16[128,24,128]{2,1,0:T(8,128)(2,1)S(1)}, u32[]{:S(2)}, u32[]{:S(2)}) async-start(bf16[128,24,128]{2,1,0:T(8,128)(2,1)} %bitcast.6), calls=%async_computation.1 | async-start | bytes 1572864 | tf_op jit(solution)/shard_map/all_to_all | solution.py:212
  40.4 0.0 copy-done
  40.4 0.6 shard_map.88
  41.1 0.0 copy-start.1
  41.1 1.2 copy-done.1
  42.2 24.2 %all-to-all-done.1 = bf16[128,24,128]{2,1,0:T(8,128)(2,1)S(1)} async-done(((bf16[128,24,128]{2,1,0:T(8,128)(2,1)}), bf16[128,24,128]{2,1,0:T(8,128)(2,1)S(1)}, u32[]{:S(2)}, u32[]{:S(2)}) %all-to-all-start.1) | async-done | bytes 786464 | tf_op jit(solution)/shard_map/all_to_all | solution.py:212
  66.4 1.3 %shard_map.89 = (bf16[4,128,1024]{2,1,0:T(8,128)(2,1)S(1)}, bf16[2,768,128]{2,1,0:T(8,128)(2,1)S(1)}) custom-call(bf16[3072,128]{1,0:T(8,128)(2,1)S(1)} %bitcast.16, s32[4,768]{1,0:T(4,128)S(1)} %get-tuple-element.20.cols_ref, bf16[768,1024]{1,0:T(8,128)(2,1)S(1)} %copy-done), custom_call_target="tpu_custom_call" | custom-call | flops 268435456 | bytes 1048576 | tf_op jit(solution)/shard_map/pallas_call | solution.py:258
  67.8 0.0 copy-start.2
  67.8 0.0 copy-start.3
  67.8 0.0 copy-start.4
  67.8 0.0 copy-start.5
  67.8 18.8 %all_to_all.39.pre_ref = bf16[4,128,1024]{2,1,0:T(8,128)(2,1)S(1)} all-to-all(bf16[4,128,1024]{2,1,0:T(8,128)(2,1)S(1)} %get-tuple-element.21), channel_id=1, replica_groups=mesh['rows'=128,'grp'=4] {'grp'}, dimensions={0} | all-to-all | bytes 2097152 | tf_op jit(solution)/shard_map/all_to_all | solution.py:212
  86.6 0.0 copy-done.2
  86.6 0.0 copy-done.3
  86.6 0.0 copy-done.4
  86.6 0.0 copy-done.5
  86.6 2.0 %shard_map.90 = (bf16[3072,128]{1,0:T(8,128)(2,1)S(1)}, f32[1,32]{1,0:T(1,128)}) custom-call(bf16[4,128,1024]{2,1,0:T(8,128)(2,1)S(1)} %all_to_all.39.pre_ref, f32[1,1024]{1,0:T(1,128)S(1)} %bitcast.20, f32[1,1024]{1,0:T(1,128)S(1)} %bitcast.21, s32[1,128]{1,0:T(1,128)S(1)} %bitcast.22, bf16[1024,768]{1,0:T(8,128)(2,1)S(1)} %copy-done.2, ...), custom_call_target="tpu_custom_call" | custom-call | flops 268435456 | bytes 1048576 | tf_op jit(solution)/shard_map/pallas_call | solution.py:265
  88.7 32.0 %all_to_all.40 = bf16[128,24,128]{2,1,0:T(8,128)(2,1)S(1)} all-to-all(bf16[128,24,128]{2,1,0:T(8,128)(2,1)S(1)} %bitcast.17), channel_id=1, replica_groups=mesh['rows'=128,'grp'=4] {'rows'}, dimensions={0} | all-to-all | bytes 1572864 | tf_op jit(solution)/shard_map/all_to_all | solution.py:212
  120.7 1.7 %shard_map.91 = f32[3,512,128]{2,1,0:T(8,128)} custom-call(s32[3,1024]{1,0:T(4,128)S(1)} %get-tuple-element.16.asked_ref, bf16[3072,128]{1,0:T(8,128)(2,1)S(1)} %bitcast.15), custom_call_target="tpu_custom_call" | custom-call | flops 268435456 | bytes 1048576 | tf_op jit(solution)/shard_map/pallas_call | solution.py:279
Async XLA Ops:
  3.0 37.4 %copy-start = (bf16[768,1024]{1,0:T(8,128)(2,1)S(1)}, bf16[768,1024]{1,0:T(8,128)(2,1)}, u32[]{:S(2)}) copy-start(bf16[768,1024]{1,0:T(8,128)(2,1)} %w_ref.3) | copy-start | bytes 4718596
  34.6 31.8 %all-to-all-start.1 = ((bf16[128,24,128]{2,1,0:T(8,128)(2,1)}), bf16[128,24,128]{2,1,0:T(8,128)(2,1)S(1)}, u32[]{:S(2)}, u32[]{:S(2)}) async-start(bf16[128,24,128]{2,1,0:T(8,128)(2,1)} %bitcast.6), calls=%async_computation.1 | async-start | bytes 1572864 | tf_op jit(solution)/shard_map/all_to_all | solution.py:212
  41.1 1.2 copy-start.1
  67.8 18.8 %copy-start.2 = (bf16[1024,768]{1,0:T(8,128)(2,1)S(1)}, bf16[1024,768]{1,0:T(8,128)(2,1)}, u32[]{:S(2)}) copy-start(bf16[1024,768]{1,0:T(8,128)(2,1)} %copy-done.1) | copy-start | bytes 4718596
  67.8 18.8 %copy-start.3 = (f32[1024]{0:T(1024)S(1)}, f32[1024]{0:T(1024)}, u32[]{:S(2)}) copy-start(f32[1024]{0:T(1024)} %param.11) | copy-start | bytes 12292
  67.8 18.8 %copy-start.4 = (f32[1024]{0:T(1024)S(1)}, f32[1024]{0:T(1024)}, u32[]{:S(2)}) copy-start(f32[1024]{0:T(1024)} %param.12) | copy-start | bytes 12292
  67.8 18.8 %copy-start.5 = (s32[128]{0:T(128)S(1)}, s32[128]{0:T(128)}, u32[]{:S(2)}) copy-start(s32[128]{0:T(128)} %param.13) | copy-start | bytes 1540

commit v6 on v5

--- a/solution.py
+++ b/solution.py
@@ -97,20 +97,7 @@
     copies[2].wait()
 
 
-def prepare_kernel(keys_ref, rank_ref, w_ref, cols_ref, wt_ref):
-    rows_dev = rank_ref.shape[0]
-    n_owner = rank_ref.shape[1] // 3
-    for k in range(3):
-        owner = keys_ref[k : k + 1, :]
-        offset_hot = one_hot(rows_dev, keys_ref[k + 3 : k + 4, :])
-        at_owner = dot(rank_ref[:, k * n_owner : (k + 1) * n_owner], offset_hot, 0, 0)
-        slot = jnp.sum(one_hot(n_owner, owner).astype(F32) * at_owner, axis=0, keepdims=True)
-        cols_ref[k : k + 1, :] = owner * SLOTS + slot.astype(jnp.int32)
-    cols_ref[3:4, :] = keys_ref[6:7, :]
-    wt_ref[...] = w_ref[...].T
-
-
-def fetch_kernel(codes_ref, table_ref, out_ref, asked_ref):
+def fetch_kernel(codes_ref, table_ref, keys_ref, rank_ref, out_ref, asked_ref, cols_ref):
     n_src = codes_ref.shape[0]
     rows_dev, width = table_ref.shape[1:]
     n_ask = n_src * SLOTS
@@ -123,16 +110,22 @@
     mine = iota((SLOTS, n_ask), 0) == iota((SLOTS, n_ask), 1) % SLOTS
     parts = []
     for k in range(3):
+        owner = keys_ref[k : k + 1, :]
+        offset_hot = one_hot(rows_dev, keys_ref[k + 3 : k + 4, :])
+        at_owner = dot(rank_ref[:, k * n_src : (k + 1) * n_src], offset_hot, 0, 0)
+        slot = jnp.sum(one_hot(n_src, owner).astype(F32) * at_owner, axis=0, keepdims=True)
+        cols_ref[k : k + 1, :] = owner * SLOTS + slot.astype(jnp.int32)
         asked = jnp.where(mine, wide[k * SLOTS : (k + 1) * SLOTS], 0.0)
         asked = jnp.sum(asked, axis=0, keepdims=True).astype(jnp.int32) - 1
         asked_ref[k : k + 1, :] = asked
         rows = dot(table_ref[k].astype(BF16), one_hot(rows_dev, asked), 0, 0).T
         parts.append(rows.reshape(n_src, SLOTS, width))
+    cols_ref[3:4, :] = keys_ref[6:7, :]
     rows = jnp.concatenate(parts, axis=1)
     out_ref[...] = rows.reshape(n_ask * 3, width).astype(BF16)
 
 
-def forward_kernel(rows_ref, cols_ref, w_ref, pre_ref, looked_ref):
+def forward_kernel(rows_ref, cols_ref, w_ref, pre_ref, looked_ref, turned_ref):
     width = rows_ref.shape[1]
     n_look = cols_ref.shape[1]
     n_owner = rows_ref.shape[0] // (3 * SLOTS)
@@ -148,6 +141,7 @@
     emb = (looked[0] * looked[1] + looked[2]).astype(BF16)
     n_b = n_look // n_feat
     emb = jnp.concatenate([emb[:, f * n_b : (f + 1) * n_b] for f in range(n_feat)], axis=0)
+    turned_ref[...] = w_ref[...].T
     pre = dot(emb, w_ref[...], 0, 0).astype(BF16)
     for g in range(pre_ref.shape[0]):
         pre_ref[g] = pre
@@ -240,24 +234,24 @@
         pltpu.with_memory_space_constraint(tables, pltpu.HBM),
         lax.axis_index("grp").astype(jnp.int32).reshape(1),
     )
-    cols, w_turned = call(
-        prepare_kernel,
-        (shape((4, n_look), jnp.int32), shape((hidden, n_feat * width), BF16)),
-        n_in=3,
-    )(keys, rank, w_first)
     requests = exchange(asked, "rows")
-    rows, asked = call(
+    rows, asked, cols = call(
         fetch_kernel,
         (
             shape((n_rows * 3 * SLOTS, width), BF16),
             shape((3, n_rows * SLOTS), jnp.int32),
-        ),
-        n_in=2,
-    )(requests, table)
+            shape((4, n_look), jnp.int32),
+        ),
+        n_in=4,
+    )(requests, table, keys, rank)
     rows = exchange(rows, "rows")
-    pre, looked = call(
+    pre, looked, w_turned = call(
         forward_kernel,
-        (shape((n_grp, n_b, hidden), BF16), shape((2, n_look, width), BF16)),
+        (
+            shape((n_grp, n_b, hidden), BF16),
+            shape((2, n_look, width), BF16),
+            shape((hidden, n_feat * width), BF16),
+        ),
         n_in=3,
     )(rows, cols, w_first)
     pre = exchange(pre, "grp")

time: 123 us -> 121 us (0.984)
  blocking collectives: 80.6 us -> 112 us
  waiting for transfers between devices: 24.2 us -> 0 us
  starting transfers between devices: 5.75 us -> 0 us
    all_to_all x3 -> x4, blocking collectives: 80.6 us -> 112 us  [exchange(): return lax.all_to_all(array, axis, split_axis=0, concat_axis=0, tiled=True)]
    all_to_all x1 -> x0, waiting for transfers between devices: 24.2 us -> none  [exchange(): return lax.all_to_all(array, axis, split_axis=0, concat_axis=0, tiled=True)]
    all_to_all x1 -> x0, starting transfers between devices: 5.75 us -> none  [exchange(): return lax.all_to_all(array, axis, split_axis=0, concat_axis=0, tiled=True)]
  transfers between devices with their start and end apart: 1 -> 0, of which waited for: 1 -> 0; matrix products, arithmetic and copies ran while one was open for 0% -> 0% of each run, Pallas kernels for 1% -> 0%
where the time goes in v6:
time: 121 us
  blocking collectives  112 us (93%)
  Pallas kernels  8.68 us (7%)
    all_to_all x4, blocking collectives, exchange(): return lax.all_to_all(array, axis, split_axis=0, concat_axis=0, tiled=True)  112 us

profile of v6, /device:TPU:1, one launch (start us, length us, event | category | flops | bytes accessed | tf_op | source)
XLA Modules:
  0.0 121.1 jit_solution(2257210177413091341)
XLA Ops:
  0.6 2.3 %shard_map.86 = (s32[128,128]{1,0:T(8,128)S(1)}, s32[7,768]{1,0:T(8,128)S(1)}, bf16[512,384]{1,0:T(8,128)(2,1)S(1)}, f32[3,512,128]{2,1,0:T(8,128)S(1)}) custom-call(s32[6,3,128]{2,1,0:T(4,128)} %bitcast.24, s32[6,3,128]{2,1,0:T(4,128)} %bitcast.25, f32[3,512,128]{2,1,0:T(8,128)} %table_hbm.1, s32[1]{0:T(128)} %bitcast.2.grp_ref), custom_call_target="tpu_custom_call" | custom-call | flops 268435456 | bytes 1048576 | tf_op jit(solution)/shard_map/pallas_call | solution.py:217
  3.0 0.0 copy-start
  3.0 29.8 %all_to_all.38 = s32[128,1,128]{2,1,0:T(1,128)S(1)} all-to-all(s32[128,1,128]{2,1,0:T(1,128)S(1)} %bitcast.20), channel_id=1, replica_groups=mesh['rows'=128,'grp'=4] {'rows'}, dimensions={0} | all-to-all | bytes 131072 | tf_op jit(solution)/shard_map/all_to_all | solution.py:206
  32.8 1.2 shard_map.87
  34.0 31.1 %all_to_all.39 = bf16[128,24,128]{2,1,0:T(8,128)(2,1)S(1)} all-to-all(bf16[128,24,128]{2,1,0:T(8,128)(2,1)S(1)} %bitcast.17), channel_id=1, replica_groups=mesh['rows'=128,'grp'=4] {'rows'}, dimensions={0} | all-to-all | bytes 1572864 | tf_op jit(solution)/shard_map/all_to_all | solution.py:206
  65.1 0.0 copy-done
  65.1 1.4 %shard_map.88 = (bf16[4,128,1024]{2,1,0:T(8,128)(2,1)S(1)}, bf16[2,768,128]{2,1,0:T(8,128)(2,1)S(1)}, bf16[1024,768]{1,0:T(8,128)(2,1)S(1)}) custom-call(bf16[3072,128]{1,0:T(8,128)(2,1)S(1)} %bitcast.16, s32[4,768]{1,0:T(4,128)S(1)} %get-tuple-element.20.cols_ref, bf16[768,1024]{1,0:T(8,128)(2,1)S(1)} %copy-done), custom_call_target="tpu_custom_call" | custom-call | flops 268435456 | bytes 1048576 | tf_op jit(solution)/shard_map/pallas_call | solution.py:248
  66.6 0.0 copy-start.1
  66.6 0.0 copy-start.2
  66.6 0.0 copy-start.3
  66.6 18.8 %all_to_all.40.pre_ref = bf16[4,128,1024]{2,1,0:T(8,128)(2,1)S(1)} all-to-all(bf16[4,128,1024]{2,1,0:T(8,128)(2,1)S(1)} %get-tuple-element.21), channel_id=1, replica_groups=mesh['rows'=128,'grp'=4] {'grp'}, dimensions={0} | all-to-all | bytes 2097152 | tf_op jit(solution)/shard_map/all_to_all | solution.py:206
  85.4 0.0 copy-done.1
  85.4 0.0 copy-done.2
  85.4 0.0 copy-done.3
  85.4 2.1 %shard_map.89 = (bf16[3072,128]{1,0:T(8,128)(2,1)S(1)}, f32[1,32]{1,0:T(1,128)}) custom-call(bf16[4,128,1024]{2,1,0:T(8,128)(2,1)S(1)} %all_to_all.40.pre_ref, f32[1,1024]{1,0:T(1,128)S(1)} %bitcast.21, f32[1,1024]{1,0:T(1,128)S(1)} %bitcast.22, s32[1,128]{1,0:T(1,128)S(1)} %bitcast.23, bf16[1024,768]{1,0:T(8,128)(2,1)S(1)} %get-tuple-element.22.w_ref, ...), custom_call_target="tpu_custom_call" | custom-call | flops 268435456 | bytes 1048576 | tf_op jit(solution)/shard_map/pallas_call | solution.py:259
  87.4 32.0 %all_to_all.41 = bf16[128,24,128]{2,1,0:T(8,128)(2,1)S(1)} all-to-all(bf16[128,24,128]{2,1,0:T(8,128)(2,1)S(1)} %bitcast.18), channel_id=1, replica_groups=mesh['rows'=128,'grp'=4] {'rows'}, dimensions={0} | all-to-all | bytes 1572864 | tf_op jit(solution)/shard_map/all_to_all | solution.py:206
  119.4 1.7 %shard_map.90 = f32[3,512,128]{2,1,0:T(8,128)} custom-call(s32[3,1024]{1,0:T(4,128)S(1)} %get-tuple-element.18.asked_ref, bf16[3072,128]{1,0:T(8,128)(2,1)S(1)} %bitcast.15), custom_call_target="tpu_custom_call" | custom-call | flops 268435456 | bytes 1048576 | tf_op jit(solution)/shard_map/pallas_call | solution.py:273
Async XLA Ops:
  3.0 62.2 %copy-start = (bf16[768,1024]{1,0:T(8,128)(2,1)S(1)}, bf16[768,1024]{1,0:T(8,128)(2,1)}, u32[]{:S(2)}) copy-start(bf16[768,1024]{1,0:T(8,128)(2,1)} %w_ref.1) | copy-start | bytes 4718596
  66.6 18.8 %copy-start.1 = (f32[1024]{0:T(1024)S(1)}, f32[1024]{0:T(1024)}, u32[]{:S(2)}) copy-start(f32[1024]{0:T(1024)} %param.11) | copy-start | bytes 12292
  66.6 18.8 %copy-start.2 = (f32[1024]{0:T(1024)S(1)}, f32[1024]{0:T(1024)}, u32[]{:S(2)}) copy-start(f32[1024]{0:T(1024)} %param.12) | copy-start | bytes 12292
  66.6 18.8 %copy-start.3 = (s32[128]{0:T(128)S(1)}, s32[128]{0:T(128)}, u32[]{:S(2)}) copy-start(s32[128]{0:T(128)} %param.13) | copy-start | bytes 1540

commit v7 on v6

--- a/solution.py
+++ b/solution.py
@@ -143,30 +143,32 @@
     emb = jnp.concatenate([emb[:, f * n_b : (f + 1) * n_b] for f in range(n_feat)], axis=0)
     turned_ref[...] = w_ref[...].T
     pre = dot(emb, w_ref[...], 0, 0).astype(BF16)
-    for g in range(pre_ref.shape[0]):
-        pre_ref[g] = pre
-
-
-def backward_kernel(
-    pre_ref, b_ref, w_out_ref, labels_ref, w_ref, cols_ref, looked_ref, out_ref, loss_ref
-):
-    n_grp, n_b, _ = pre_ref.shape
+    pre_ref[...] = pre
+
+
+def head_kernel(pre_ref, b_ref, w_out_ref, labels_ref, cols_ref, grad_ref, loss_ref):
+    n_grp, share, _ = pre_ref.shape
+    n_b = labels_ref.shape[1]
     pre = b_ref[...]
     for g in range(n_grp):
         pre = pre + pre_ref[g].astype(F32)
     w_out = w_out_ref[...]
     sig = jax.nn.sigmoid(pre)
     logits = jnp.sum(pre * sig * w_out, axis=1, keepdims=True)
-    diagonal = iota((n_b, n_b), 0) == iota((n_b, n_b), 1)
-    targets = jnp.sum(jnp.where(diagonal, labels_ref[...].astype(F32), 0.0), axis=1, keepdims=True)
+    mine = iota((share, n_b), 1) == iota((share, n_b), 0) + cols_ref[3:4, :n_b] * share
+    targets = jnp.sum(jnp.where(mine, labels_ref[...].astype(F32), 0.0), axis=1, keepdims=True)
     soft = jnp.maximum(logits, 0.0) + jnp.log1p(jnp.exp(-jnp.abs(logits)))
     losses = soft - targets * logits
-    share = loss_ref.shape[1]
-    mine = iota((n_b, share), 0) == iota((n_b, share), 1) + cols_ref[3:4, :share] * share
-    loss_ref[...] = jnp.sum(jnp.where(mine, losses, 0.0), axis=0, keepdims=True)
+    diagonal = iota((share, share), 0) == iota((share, share), 1)
+    loss_ref[...] = jnp.sum(jnp.where(diagonal, losses, 0.0), axis=0, keepdims=True)
     grad_logit = jax.nn.sigmoid(logits) - targets
     grad = (grad_logit * w_out * (sig * (1.0 + pre * (1.0 - sig)))).astype(BF16)
-
+    for g in range(n_grp):
+        grad_ref[g] = grad
+
+
+def backward_kernel(grad_ref, w_ref, cols_ref, looked_ref, out_ref):
+    grad = grad_ref[...]
     width = out_ref.shape[1]
     n_look = cols_ref.shape[1]
     n_owner = out_ref.shape[0] // (3 * SLOTS)
@@ -248,26 +250,22 @@
     pre, looked, w_turned = call(
         forward_kernel,
         (
-            shape((n_grp, n_b, hidden), BF16),
+            shape((n_b, hidden), BF16),
             shape((2, n_look, width), BF16),
             shape((hidden, n_feat * width), BF16),
         ),
         n_in=3,
     )(rows, cols, w_first)
-    pre = exchange(pre, "grp")
     share = n_b // n_grp
-    sums, losses = call(
-        backward_kernel,
-        (shape((n_rows * 3 * SLOTS, width), BF16), shape((1, share), F32)),
-        n_in=7,
-    )(
-        pre,
-        b_first.reshape(1, hidden),
-        w_out.reshape(1, hidden),
-        labels.reshape(1, n_b),
-        w_turned,
-        cols,
-        looked,
+    pre = exchange(pre.reshape(n_grp, share, hidden), "grp")
+    grad, losses = call(
+        head_kernel,
+        (shape((n_grp, share, hidden), BF16), shape((1, share), F32)),
+        n_in=5,
+    )(pre, b_first.reshape(1, hidden), w_out.reshape(1, hidden), labels.reshape(1, n_b), cols)
+    grad = exchange(grad, "grp").reshape(n_b, hidden)
+    sums = call(backward_kernel, shape((n_rows * 3 * SLOTS, width), BF16), n_in=4)(
+        grad, w_turned, cols, looked
     )
     sums = exchange(sums, "rows")
     table_grad = call(

time: 121 us -> 122 us (level)
    all_to_all x4 -> x5, blocking collectives: 112 us -> 112 us  [exchange(): return lax.all_to_all(array, axis, split_axis=0, concat_axis=0, tiled=True)]
    pallas_call x2 -> x3, Pallas kernels: 3.47 us -> 3.84 us  [the longest x1 1.75 us: body(): call(backward_kernel, shape((n_rows * 3 * SLOTS, width), BF16), n_in=4)]
where the time goes in v7:
time: 122 us
  blocking collectives  112 us (92%)
  Pallas kernels  9.05 us (7%)
    all_to_all x5, blocking collectives, exchange(): return lax.all_to_all(array, axis, split_axis=0, concat_axis=0, tiled=True)  112 us

profile of v7, /device:TPU:1, one launch (start us, length us, event | category | flops | bytes accessed | tf_op | source)
XLA Modules:
  0.0 121.9 jit_solution(3573160097097892452)
XLA Ops:
  0.6 2.3 %shard_map.86 = (s32[128,128]{1,0:T(8,128)S(1)}, s32[7,768]{1,0:T(8,128)S(1)}, bf16[512,384]{1,0:T(8,128)(2,1)S(1)}, f32[3,512,128]{2,1,0:T(8,128)S(1)}) custom-call(s32[6,3,128]{2,1,0:T(4,128)} %bitcast.28, s32[6,3,128]{2,1,0:T(4,128)} %bitcast.29, f32[3,512,128]{2,1,0:T(8,128)} %table_hbm.1, s32[1]{0:T(128)} %bitcast.2.grp_ref), custom_call_target="tpu_custom_call" | custom-call | flops 268435456 | bytes 1048576 | tf_op jit(solution)/shard_map/pallas_call | solution.py:219
  3.0 0.0 copy-start
  3.0 29.8 %all_to_all.43 = s32[128,1,128]{2,1,0:T(1,128)S(1)} all-to-all(s32[128,1,128]{2,1,0:T(1,128)S(1)} %bitcast.24), channel_id=1, replica_groups=mesh['rows'=128,'grp'=4] {'rows'}, dimensions={0} | all-to-all | bytes 131072 | tf_op jit(solution)/shard_map/all_to_all | solution.py:208
  32.8 1.2 shard_map.87
  34.0 31.1 %all_to_all.44 = bf16[128,24,128]{2,1,0:T(8,128)(2,1)S(1)} all-to-all(bf16[128,24,128]{2,1,0:T(8,128)(2,1)S(1)} %bitcast.21), channel_id=1, replica_groups=mesh['rows'=128,'grp'=4] {'rows'}, dimensions={0} | all-to-all | bytes 1572864 | tf_op jit(solution)/shard_map/all_to_all | solution.py:208
  65.1 0.0 copy-start.1
  65.1 0.0 copy-start.2
  65.1 0.0 copy-start.3
  65.1 0.0 copy-done
  65.1 1.4 %shard_map.88 = (bf16[128,1024]{1,0:T(8,128)(2,1)S(1)}, bf16[2,768,128]{2,1,0:T(8,128)(2,1)S(1)}, bf16[1024,768]{1,0:T(8,128)(2,1)S(1)}) custom-call(bf16[3072,128]{1,0:T(8,128)(2,1)S(1)} %bitcast.18, s32[4,768]{1,0:T(4,128)S(1)} %get-tuple-element.20.cols_ref, bf16[768,1024]{1,0:T(8,128)(2,1)S(1)} %copy-done), custom_call_target="tpu_custom_call" | custom-call | flops 268435456 | bytes 1048576 | tf_op jit(solution)/shard_map/pallas_call | solution.py:250
  66.5 10.2 %all_to_all.45.pre_ref = bf16[4,32,1024]{2,1,0:T(8,128)(2,1)S(1)} all-to-all(bf16[4,32,1024]{2,1,0:T(8,128)(2,1)S(1)} %bitcast.23), channel_id=1, replica_groups=mesh['rows'=128,'grp'=4] {'grp'}, dimensions={0} | all-to-all | bytes 524288 | tf_op jit(solution)/shard_map/all_to_all | solution.py:208
  76.7 0.0 copy-done.1
  76.7 0.0 copy-done.2
  76.7 0.0 copy-done.3
  76.7 0.7 shard_map.89
  77.4 7.9 %all_to_all.46 = bf16[4,32,1024]{2,1,0:T(8,128)(2,1)S(1)} all-to-all(bf16[4,32,1024]{2,1,0:T(8,128)(2,1)S(1)} %get-tuple-element.22), channel_id=1, replica_groups=mesh['rows'=128,'grp'=4] {'grp'}, dimensions={0} | all-to-all | bytes 524288 | tf_op jit(solution)/shard_map/all_to_all | solution.py:208
  85.3 1.8 %shard_map.90 = bf16[3072,128]{1,0:T(8,128)(2,1)S(1)} custom-call(bf16[128,1024]{1,0:T(8,128)(2,1)S(1)} %bitcast.20, bf16[1024,768]{1,0:T(8,128)(2,1)S(1)} %get-tuple-element.23.w_ref, s32[4,768]{1,0:T(4,128)S(1)} %get-tuple-element.20.cols_ref, bf16[2,768,128]{2,1,0:T(8,128)(2,1)S(1)} %get-tuple-element.24.looked_ref), custom_call_target="tpu_custom_call" | custom-call | flops 268435456 | bytes 1048576 | tf_op jit(solution)/shard_map/pallas_call | solution.py:267
  87.1 33.1 %all_to_all.47 = bf16[128,24,128]{2,1,0:T(8,128)(2,1)S(1)} all-to-all(bf16[128,24,128]{2,1,0:T(8,128)(2,1)S(1)} %bitcast.19), channel_id=1, replica_groups=mesh['rows'=128,'grp'=4] {'rows'}, dimensions={0} | all-to-all | bytes 1572864 | tf_op jit(solution)/shard_map/all_to_all | solution.py:208
  120.2 1.7 %shard_map.91 = f32[3,512,128]{2,1,0:T(8,128)} custom-call(s32[3,1024]{1,0:T(4,128)S(1)} %get-tuple-element.18.asked_ref, bf16[3072,128]{1,0:T(8,128)(2,1)S(1)} %bitcast.17), custom_call_target="tpu_custom_call" | custom-call | flops 268435456 | bytes 1048576 | tf_op jit(solution)/shard_map/pallas_call | solution.py:271
Async XLA Ops:
  3.0 62.2 %copy-start = (bf16[768,1024]{1,0:T(8,128)(2,1)S(1)}, bf16[768,1024]{1,0:T(8,128)(2,1)}, u32[]{:S(2)}) copy-start(bf16[768,1024]{1,0:T(8,128)(2,1)} %w_ref.1) | copy-start | bytes 4718596
  65.1 11.6 %copy-start.1 = (f32[1024]{0:T(1024)S(1)}, f32[1024]{0:T(1024)}, u32[]{:S(2)}) copy-start(f32[1024]{0:T(1024)} %param.11) | copy-start | bytes 12292
  65.1 11.6 %copy-start.2 = (f32[1024]{0:T(1024)S(1)}, f32[1024]{0:T(1024)}, u32[]{:S(2)}) copy-start(f32[1024]{0:T(1024)} %param.12) | copy-start | bytes 12292
  65.1 11.6 %copy-start.3 = (s32[128]{0:T(128)S(1)}, s32[128]{0:T(128)}, u32[]{:S(2)}) copy-start(s32[128]{0:T(128)} %param.13) | copy-start | bytes 1540

commit v8 on v6

--- a/solution.py
+++ b/solution.py
@@ -72,8 +72,7 @@
         owner = jnp.concatenate([owner_ref[f, k : k + 1, :] for f in range(n_feat)], axis=1)
         offset = jnp.concatenate([offset_ref[f, k : k + 1, :] for f in range(n_feat)], axis=1)
         pairs.append((owner, offset, one_hot(n_owner, owner), one_hot(rows_dev, offset)))
-    by_look = [owner_hot.T for _, _, owner_hot, _ in pairs]
-    present = jnp.concatenate([dot(pairs[k][3], by_look[k], 1, 0) for k in range(3)], axis=1)
+    present = jnp.concatenate([dot(pairs[k][3], pairs[k][2], 1, 1) for k in range(3)], axis=1)
     rank = dot(before, jnp.minimum(present, 1.0).astype(BF16), 1, 0).astype(BF16)
     rank_ref[...] = rank
     asked = []
@@ -118,7 +117,7 @@
         asked = jnp.where(mine, wide[k * SLOTS : (k + 1) * SLOTS], 0.0)
         asked = jnp.sum(asked, axis=0, keepdims=True).astype(jnp.int32) - 1
         asked_ref[k : k + 1, :] = asked
-        rows = dot(table_ref[k].astype(BF16), one_hot(rows_dev, asked), 0, 0).T
+        rows = dot(table_ref[k].astype(BF16), one_hot(rows_dev, asked), 0, 0).astype(BF16).T.astype(F32)
         parts.append(rows.reshape(n_src, SLOTS, width))
     cols_ref[3:4, :] = keys_ref[6:7, :]
     rows = jnp.concatenate(parts, axis=1)
@@ -136,8 +135,8 @@
         mine = rows[:, k * SLOTS : (k + 1) * SLOTS, :].reshape(n_owner * SLOTS, width).astype(BF16)
         onehot = one_hot(n_owner * SLOTS, cols_ref[k : k + 1, :])
         looked.append(dot(mine, onehot, 0, 0))
-    looked_ref[0] = looked[0].T.astype(BF16)
-    looked_ref[1] = looked[1].T.astype(BF16)
+    looked_ref[0] = looked[0].astype(BF16).T
+    looked_ref[1] = looked[1].astype(BF16).T
     emb = (looked[0] * looked[1] + looked[2]).astype(BF16)
     n_b = n_look // n_feat
     emb = jnp.concatenate([emb[:, f * n_b : (f + 1) * n_b] for f in range(n_feat)], axis=0)
@@ -193,10 +192,10 @@
     copies = []
     for k in range(3):
         mine = grads[:, k * SLOTS : (k + 1) * SLOTS, :].reshape(n_ask, width).astype(BF16)
-        for h in range(2):
-            half = pl.ds(h * rows_dev // 2, rows_dev // 2)
-            out_ref[k, half] = dot(one_hot(rows_dev // 2, asked_ref[k : k + 1, :] - h * rows_dev // 2), mine, 1, 0)
-            copies.append(pltpu.make_async_copy(out_ref.at[k, half], out_hbm.at[k, half], sems.at[2 * k + h]))
+        for h in range(4):
+            half = pl.ds(h * rows_dev // 4, rows_dev // 4)
+            out_ref[k, half] = dot(one_hot(rows_dev // 4, asked_ref[k : k + 1, :] - h * rows_dev // 4), mine, 1, 0)
+            copies.append(pltpu.make_async_copy(out_ref.at[k, half], out_hbm.at[k, half], sems.at[4 * k + h]))
             copies[-1].start()
     for copy in copies:
         copy.wait()
@@ -275,7 +274,7 @@
         shape((3, rows_dev, width), F32),
         n_in=2,
         out=pltpu.HBM,
-        scratch=(pltpu.VMEM((3, rows_dev, width), F32), pltpu.SemaphoreType.DMA((6,))),
+        scratch=(pltpu.VMEM((3, rows_dev, width), F32), pltpu.SemaphoreType.DMA((12,))),
     )(asked, sums)
     return table_grad, losses.reshape(share)
 

time: 121 us -> 121 us (level)
  no operation moved by 1% of the time
where the time goes in v8:
time: 121 us
  blocking collectives  112 us (93%)
  Pallas kernels  8.69 us (7%)
    all_to_all x4, blocking collectives, exchange(): return lax.all_to_all(array, axis, split_axis=0, concat_axis=0, tiled=True)  112 us

profile of v8, /device:TPU:1, one launch (start us, length us, event | category | flops | bytes accessed | tf_op | source)
XLA Modules:
  0.0 121.1 jit_solution(12198754199692669312)
XLA Ops:
  0.6 2.3 %shard_map.86 = (s32[128,128]{1,0:T(8,128)S(1)}, s32[7,768]{1,0:T(8,128)S(1)}, bf16[512,384]{1,0:T(8,128)(2,1)S(1)}, f32[3,512,128]{2,1,0:T(8,128)S(1)}) custom-call(s32[6,3,128]{2,1,0:T(4,128)} %bitcast.24, s32[6,3,128]{2,1,0:T(4,128)} %bitcast.25, f32[3,512,128]{2,1,0:T(8,128)} %table_hbm.1, s32[1]{0:T(128)} %bitcast.2.grp_ref), custom_call_target="tpu_custom_call" | custom-call | flops 268435456 | bytes 1048576 | tf_op jit(solution)/shard_map/pallas_call | solution.py:216
  3.0 0.0 copy-start
  3.0 29.8 %all_to_all.38 = s32[128,1,128]{2,1,0:T(1,128)S(1)} all-to-all(s32[128,1,128]{2,1,0:T(1,128)S(1)} %bitcast.20), channel_id=1, replica_groups=mesh['rows'=128,'grp'=4] {'rows'}, dimensions={0} | all-to-all | bytes 131072 | tf_op jit(solution)/shard_map/all_to_all | solution.py:205
  32.8 1.2 shard_map.87
  34.0 31.1 %all_to_all.39 = bf16[128,24,128]{2,1,0:T(8,128)(2,1)S(1)} all-to-all(bf16[128,24,128]{2,1,0:T(8,128)(2,1)S(1)} %bitcast.17), channel_id=1, replica_groups=mesh['rows'=128,'grp'=4] {'rows'}, dimensions={0} | all-to-all | bytes 1572864 | tf_op jit(solution)/shard_map/all_to_all | solution.py:205
  65.1 0.0 copy-done
  65.1 1.4 %shard_map.88 = (bf16[4,128,1024]{2,1,0:T(8,128)(2,1)S(1)}, bf16[2,768,128]{2,1,0:T(8,128)(2,1)S(1)}, bf16[1024,768]{1,0:T(8,128)(2,1)S(1)}) custom-call(bf16[3072,128]{1,0:T(8,128)(2,1)S(1)} %bitcast.16, s32[4,768]{1,0:T(4,128)S(1)} %get-tuple-element.20.cols_ref, bf16[768,1024]{1,0:T(8,128)(2,1)S(1)} %copy-done), custom_call_target="tpu_custom_call" | custom-call | flops 268435456 | bytes 1048576 | tf_op jit(solution)/shard_map/pallas_call | solution.py:247
  66.6 0.0 copy-start.1
  66.6 0.0 copy-start.2
  66.6 0.0 copy-start.3
  66.6 18.7 %all_to_all.40.pre_ref = bf16[4,128,1024]{2,1,0:T(8,128)(2,1)S(1)} all-to-all(bf16[4,128,1024]{2,1,0:T(8,128)(2,1)S(1)} %get-tuple-element.21), channel_id=1, replica_groups=mesh['rows'=128,'grp'=4] {'grp'}, dimensions={0} | all-to-all | bytes 2097152 | tf_op jit(solution)/shard_map/all_to_all | solution.py:205
  85.3 0.0 copy-done.1
  85.3 0.0 copy-done.2
  85.3 0.0 copy-done.3
  85.3 2.0 %shard_map.89 = (bf16[3072,128]{1,0:T(8,128)(2,1)S(1)}, f32[1,32]{1,0:T(1,128)}) custom-call(bf16[4,128,1024]{2,1,0:T(8,128)(2,1)S(1)} %all_to_all.40.pre_ref, f32[1,1024]{1,0:T(1,128)S(1)} %bitcast.21, f32[1,1024]{1,0:T(1,128)S(1)} %bitcast.22, s32[1,128]{1,0:T(1,128)S(1)} %bitcast.23, bf16[1024,768]{1,0:T(8,128)(2,1)S(1)} %get-tuple-element.22.w_ref, ...), custom_call_target="tpu_custom_call" | custom-call | flops 268435456 | bytes 1048576 | tf_op jit(solution)/shard_map/pallas_call | solution.py:258
  87.4 32.0 %all_to_all.41 = bf16[128,24,128]{2,1,0:T(8,128)(2,1)S(1)} all-to-all(bf16[128,24,128]{2,1,0:T(8,128)(2,1)S(1)} %bitcast.18), channel_id=1, replica_groups=mesh['rows'=128,'grp'=4] {'rows'}, dimensions={0} | all-to-all | bytes 1572864 | tf_op jit(solution)/shard_map/all_to_all | solution.py:205
  119.4 1.7 %shard_map.90 = f32[3,512,128]{2,1,0:T(8,128)} custom-call(s32[3,1024]{1,0:T(4,128)S(1)} %get-tuple-element.18.asked_ref, bf16[3072,128]{1,0:T(8,128)(2,1)S(1)} %bitcast.15), custom_call_target="tpu_custom_call" | custom-call | flops 268435456 | bytes 1048576 | tf_op jit(solution)/shard_map/pallas_call | solution.py:272
Async XLA Ops:
  3.0 62.1 %copy-start = (bf16[768,1024]{1,0:T(8,128)(2,1)S(1)}, bf16[768,1024]{1,0:T(8,128)(2,1)}, u32[]{:S(2)}) copy-start(bf16[768,1024]{1,0:T(8,128)(2,1)} %w_ref.1) | copy-start | bytes 4718596
  66.6 18.8 %copy-start.1 = (f32[1024]{0:T(1024)S(1)}, f32[1024]{0:T(1024)}, u32[]{:S(2)}) copy-start(f32[1024]{0:T(1024)} %param.11) | copy-start | bytes 12292
  66.6 18.8 %copy-start.2 = (f32[1024]{0:T(1024)S(1)}, f32[1024]{0:T(1024)}, u32[]{:S(2)}) copy-start(f32[1024]{0:T(1024)} %param.12) | copy-start | bytes 12292
  66.6 18.8 %copy-start.3 = (s32[128]{0:T(128)S(1)}, s32[128]{0:T(128)}, u32[]{:S(2)}) copy-start(s32[128]{0:T(128)} %param.13) | copy-start | bytes 1540
